TPU v7x, 256 devices: a whole 4x4x8 slice. The times are simulated.
256 devices in a mesh: context: 32 (over z, x), tensor: 8 (over y, core).
Axes of the slice: x: 4, y: 4, z: 8, core: 2. Of those that a mesh axis runs over, the one named last changes fastest.
Arguments:
- activations: bfloat16 [16384, 3072], P(('context', 'tensor')), may hold values from -6 to 6
- w_qkv: bfloat16 [3072, 3, 4096], P(None, None, 'tensor'), may hold values from -0.109375 to 0.109375
- w_out: bfloat16 [4096, 3072], P('tensor'), may hold values from -0.09375 to 0.09375
- log_decay: float32 [32, 16384], P('tensor', 'context'), may hold values from -0.7 to 0
Outputs:
- mixed: bfloat16 [16384, 3072], P(('context', 'tensor'))
All inputs are finite; a program needn't handle non-finite values.
Results may differ from a plain program's by a relative error of at most 0.02.
Values may be sent and summed in bfloat16 or wider, within the bound.
A program may use at most 128 MiB of HBM per device.

v0:
```python
import jax
import jax.numpy as jnp
from jax import lax
from jax.sharding import PartitionSpec as P

HEAD_DIM = 128
BLOCK = 256


def entering(x, axis, combine, identity):
    peers, place = (lax.axis_size(axis), lax.axis_index(axis))
    everything = jax.tree.map(lambda part: lax.all_gather(part, axis), x)
    start = jax.tree.map(
        lambda part, zero: jnp.broadcast_to(jnp.asarray(zero, part.dtype), part.shape), x, identity
    )

    def step(k, before):
        reached = k < place
        new = combine(before, jax.tree.map(lambda part: part[k], everything))
        return jax.tree.map(lambda a, b: jnp.where(reached, a, b), new, before)

    return lax.fori_loop(0, peers, step, start)


def block_step(state, items):
    queries, keys, values, decay = items
    cumulative = jnp.cumsum(decay, axis=1)
    size = decay.shape[1]
    lower = jnp.arange(size)[:, None] >= jnp.arange(size)[None, :]
    gaps = jnp.minimum(cumulative[:, :, None] - cumulative[:, None, :], 0.0)
    mask = jnp.where(lower[None], jnp.exp(gaps), 0.0)
    scores = jnp.einsum("hid,hjd->hij", queries, keys, preferred_element_type=jnp.float32)
    block_weights = (scores * mask).astype(jnp.bfloat16)
    inner = jnp.einsum("hij,hjd->hid", block_weights, values, preferred_element_type=jnp.float32)
    scaled = queries.astype(jnp.float32) * jnp.exp(cumulative)[:, :, None]
    carried = jnp.einsum("hid,hde->hie", scaled, state, precision=lax.Precision.HIGHEST)
    last = cumulative[:, -1]
    weighted_keys = keys.astype(jnp.float32) * jnp.exp(last[:, None] - cumulative)[:, :, None]
    update = jnp.einsum(
        "hjd,hje->hde", weighted_keys, values.astype(jnp.float32), precision=lax.Precision.HIGHEST
    )
    new_state = jnp.exp(last)[:, None, None] * state + update
    return (new_state, inner + carried)


def join_states(earlier, later):
    return (earlier[0] * later[0], later[0][:, None, None] * earlier[1] + later[1])


def body(activations, w_qkv, w_out, log_decay):
    resident_attention_heads = log_decay.shape[0]
    width = resident_attention_heads * HEAD_DIM
    weights_flat = w_qkv.reshape(w_qkv.shape[0], 3 * width)
    projected = jnp.dot(
        lax.all_gather(activations, "tensor", axis=0, tiled=True),
        weights_flat,
        preferred_element_type=jnp.float32,
    )
    ctx_rows = projected.shape[0]
    n_blocks = ctx_rows // BLOCK
    queries = jax.nn.silu(projected[:, :width]).astype(jnp.bfloat16)
    keys = jax.nn.silu(projected[:, width : 2 * width]).astype(jnp.bfloat16)
    values = projected[:, 2 * width :].astype(jnp.bfloat16)

    def reshape_into_blocks(array):
        return array.reshape(n_blocks, BLOCK, resident_attention_heads, HEAD_DIM).transpose(
            0, 2, 1, 3
        )

    decay_blocks = log_decay.reshape(resident_attention_heads, n_blocks, BLOCK).transpose(1, 0, 2)
    initial_memory_matrix = jnp.zeros((resident_attention_heads, HEAD_DIM, HEAD_DIM), jnp.float32)
    final_state, local_out = lax.scan(
        block_step,
        initial_memory_matrix,
        (
            reshape_into_blocks(queries),
            reshape_into_blocks(keys),
            reshape_into_blocks(values),
            decay_blocks,
        ),
    )
    local_out = local_out.transpose(1, 0, 2, 3).reshape(
        resident_attention_heads, ctx_rows, HEAD_DIM
    )
    totals = jnp.sum(log_decay, axis=1)
    unit_matrix = (jnp.ones_like(totals), jnp.zeros_like(final_state))
    _, incoming = entering((jnp.exp(totals), final_state), "context", join_states, unit_matrix)
    running = jnp.cumsum(log_decay, axis=1)
    head_queries = queries.reshape(ctx_rows, resident_attention_heads, HEAD_DIM).transpose(1, 0, 2)
    scaled = head_queries.astype(jnp.float32) * jnp.exp(running)[:, :, None]
    attended_rows = local_out + jnp.einsum(
        "hid,hde->hie", scaled, incoming, precision=lax.Precision.HIGHEST
    )
    normed = attended_rows * lax.rsqrt(
        jnp.mean(attended_rows * attended_rows, axis=2, keepdims=True) + 1e-06
    )
    flat = normed.transpose(1, 0, 2).reshape(ctx_rows, width).astype(jnp.bfloat16)
    return lax.psum_scatter(
        jnp.dot(flat, w_out, preferred_element_type=jnp.float32).astype(jnp.bfloat16),
        "tensor",
        scatter_dimension=0,
        tiled=True,
    )


def solution(mesh):
    in_specs = (
        P(("context", "tensor"), None),
        P(None, None, "tensor"),
        P("tensor", None),
        P("tensor", "context"),
    )
    out_specs = P(("context", "tensor"), None)
    return jax.shard_map(body, mesh=mesh, in_specs=in_specs, out_specs=out_specs, check_vma=False)
```

profile of v0, /device:TPU:1, one launch (start us, length us, event | category | flops | bytes accessed | tf_op | source)
XLA Modules:
  0.0 262.9 jit_solution(5336903752950109959)
XLA Ops:
  7.3 12.9 %copy.28 = bf16[3072,3,512]{0,2,1:T(8,128)(2,1)} copy(bf16[3072,3,512]{2,0,1:T(8,128)(2,1)} %param.9) | data formatting | bytes 18874368 | tf_op args[1]
  20.2 23.6 %all-gather.5.cloned.1.call-done = bf16[512,3072]{1,0:T(8,128)(2,1)} async-done(((bf16[64,3072]{1,0:T(8,128)(2,1)}), bf16[512,3072]{1,0:T(8,128)(2,1)}) %all-gather.5.cloned.1.call-update) | async-done | bytes 3145744 | tf_op jit(solution)/shard_map/all_gather | solution.py:55
  43.8 8.6 %fusion.51 = f32[512,1536]{1,0:T(8,128)S(1)} fusion(bf16[512,3072]{1,0:T(8,128)(2,1)} %all-gather.5.cloned.1.call-done, bf16[3072,1536]{0,1:T(8,128)(2,1)} %bitcast.119), kind=kOutput, calls=%fused_computation.72 | convolution fusion | flops 4831838208 | bytes 15728640 | tf_op jit(solution)/shard_map/dot_general | solution.py:54
  52.4 1.6 convert_bitcast_fusion
  54.9 2.0 reshape.148
  56.9 2.0 reshape.147
  58.8 2.0 reshape.146
  60.8 1.9 copy.57
  62.7 2.4 copy_bitcast_fusion.1
  65.1 17.8 %while.27 = (s32[]{:T(128)}, f32[4,128,128]{2,1,0:T(8,128)S(1)}, f32[2,4,256,128]{3,2,1,0:T(8,128)}, f32[2,4,256]{2,1,0:T(4,128)S(1)}, bf16[2,4,256,128]{3,2,1,0...) while((s32[]{:T(128)}, f32[4,128,128]{2,1,0:T(8,128)S(1)}, ...), condition=%wide.region_3.4_spmd.clone, body=%wide.region_0.3_spmd.clone.sunk | while | flops 539296768 | bytes 4137068 | solution.py:72
  67.0 2.5 fusion.76
  69.5 2.6 %fusion.77 = f32[2,4,256,128]{3,2,1,0:T(8,128)} fusion(f32[2,4,256,128]{3,2,1,0:T(8,128)} %get-tuple-element.305, s32[]{:T(128)} %get-tuple-element.303, f32[4,256,128]{2,1,0:T(8,128)} %fusion.76, f32[4,256]{1,0:T(4,128)S(1)} %bitcast.124, pred[256,256]{1,0:T(8,128)(4,1)S(1)} %iota_compare_fusion.2, bf16[2,4,256,128]{3,2,1,0:T(8,128)(2,1)} %get-tuple-element.319, ...), kind=kOutput, calls=%fused_computation.5.clone.1 | convolution fusion | flops 135659520 | bytes 1910784 | tf_op jit(solution)/shard_map/while/body/eval_jaxpr/hij,hjd->hid/dot_general | solution.py:34
  72.1 1.9 convolution_add_fusion.3
  75.9 2.5 fusion.76
  78.4 2.7 %fusion.77 = f32[2,4,256,128]{3,2,1,0:T(8,128)} fusion(f32[2,4,256,128]{3,2,1,0:T(8,128)} %get-tuple-element.305, s32[]{:T(128)} %get-tuple-element.303, f32[4,256,128]{2,1,0:T(8,128)} %fusion.76, f32[4,256]{1,0:T(4,128)S(1)} %bitcast.124, pred[256,256]{1,0:T(8,128)(4,1)S(1)} %iota_compare_fusion.2, bf16[2,4,256,128]{3,2,1,0:T(8,128)(2,1)} %get-tuple-element.319, ...), kind=kOutput, calls=%fused_computation.5.clone.1 | convolution fusion | flops 135659520 | bytes 1910784 | tf_op jit(solution)/shard_map/while/body/eval_jaxpr/hij,hjd->hid/dot_general | solution.py:34
  81.0 1.9 convolution_add_fusion.3
  85.2 61.5 %all-reduce = f32[128]{0:T(128)S(1)} all-reduce(f32[128]{0:T(128)S(1)} %exponential_dynamic-update-slice_fusion), channel_id=2, replica_groups=mesh['context'=32,'tensor'=8] {'context'}, use_global_device_ids=true, to_apply=%add | all-reduce | flops 128 | bytes 1024
  148.5 2.3 copy.32
  150.8 3.0 %reshape.149 = f32[4,512,128]{1,2,0:T(8,128)} reshape(f32[4,2,256,128]{2,1,3,0:T(2,128)} %copy.32) | data formatting | bytes 2097152 | tf_op jit(solution)/shard_map/reshape | solution.py:82
  153.8 27.7 %all-gather.7.cloned.1.call-done = f32[128,128,128]{2,1,0:T(8,128)} async-done(((f32[4,128,128]{2,1,0:T(8,128)}), f32[128,128,128]{2,1,0:T(8,128)}) %all-gather.7.cloned.1.call-update) | async-done | bytes 8388624 | tf_op jit(solution)/shard_map/all_gather | solution.py:12
  181.5 35.0 %while.28 = (s32[]{:T(128)}, f32[4,128,128]{2,1,0:T(8,128)S(1)}, s32[]{:T(128)}, f32[32,4]{1,0:T(8,128)S(1)}, f32[32,4,128,128]{3,2,1,0:T(8,128)}, /*index=5*/s32[]{:T(128)}, s32[]{:T(128)}) while((s32[]{:T(128)}, f32[4,128,128]{2,1,0:T(8,128)S(1)}, s32[]{:T(128)}, f32[32,4]{1,0:T(8,128)S(1)}, f32[32,4,128,128]{3,2,1,0:T(8,128)}, ...), condition=%wide.region_8.9_spmd.clone, body=%wide.region_7.8_spmd.clone.sunk | while | flops 262148 | bytes 786585 | solution.py:22
  216.5 3.0 %multiply_reduce_fusion = (f32[4,512]{1,0:T(4,128)S(1)}, f32[4,512,128]{1,2,0:T(8,128)S(1)}) fusion(f32[4,512,128]{1,2,0:T(8,128)} %reshape.149, f32[4,128,128]{2,1,0:T(8,128)S(1)} %get-tuple-element.139, f32[64,4,8,128]{3,2,1,0:T(8,128)} %get-tuple-element.206, f32[4,512]{1,0:T(4,128)S(1)} %bitcast.131), kind=kOutput, calls=%fused_computation.60 | convolution fusion | flops 403699712 | bytes 3424256 | tf_op jit(solution)/shard_map/hid,hde->hie/dot_general | solution.py:91
  219.7 3.5 %convolution_convert_fusion = bf16[512,3072]{1,0:T(8,128)(2,1)} fusion(bf16[512,512]{0,1:T(8,128)(2,1)S(1)} %bitcast.121, bf16[512,3072]{1,0:T(8,128)(2,1)S(1)} %copy-done), kind=kOutput, calls=%fused_computation.52 | convolution fusion | flops 1612185600 | bytes 6815744 | tf_op jit(solution)/shard_map/dot_general | solution.py:99
  223.2 33.2 %reduce-scatter.2.cloned.1.call-done = bf16[64,3072]{1,0:T(8,128)(2,1)} async-done(((bf16[512,3072]{1,0:T(8,128)(2,1)}), bf16[64,3072]{1,0:T(8,128)(2,1)}) %reduce-scatter.2.cloned.1.call-update) | async-done | bytes 393232 | tf_op jit(solution)/shard_map/reduce_scatter | solution.py:98
  (125 shorter events, 42.9 us)
Async XLA Ops:
  6.5 213.1 %copy-start = (bf16[512,3072]{1,0:T(8,128)(2,1)S(1)}, bf16[512,3072]{1,0:T(8,128)(2,1)}, u32[]{:S(2)}) copy-start(bf16[512,3072]{1,0:T(8,128)(2,1)} %param.10) | copy-start | bytes 9437188
  6.5 37.2 %all-gather.5.cloned.1.call-start = ((), (), s32[]{:S(2)}) async-start(), calls=%async_computation.1 | async-start | bytes 3538944 | tf_op jit(solution)/shard_map/all_gather | solution.py:55
  7.3 174.3 %all-gather.7.cloned.1.call-start = ((), (), s32[]{:S(2)}) async-start(), calls=%async_computation.3 | async-start | bytes 8650752 | tf_op jit(solution)/shard_map/all_gather | solution.py:12
  54.9 10.2 %copy-start.2 = (f32[4,512]{1,0:T(4,128)S(1)}, f32[4,512]{1,0:T(4,128)}, u32[]{:S(2)}) copy-start(f32[4,512]{1,0:T(4,128)} %param.11) | copy-start | bytes 24580
  65.1 18.7 %copy-start.3 = (u32[256]{0:T(256)S(1)}, u32[256]{0:T(256)}, u32[]{:S(2)}) copy-start(u32[256]{0:T(256)} %constant.69) | copy-start | bytes 3076
  82.9 0.7 copy-start.1
  83.6 172.7 %reduce-scatter.2.cloned.1.call-start = ((), (), s32[]{:S(2)}) async-start(), calls=%async_computation.2 | async-start | bytes 3538944 | tf_op jit(solution)/shard_map/reduce_scatter | solution.py:98
Sparse Core Ops, SparseCore 0:
  9.2 34.5 all-gather.4
  83.8 97.7 all-gather.6
  223.3 33.0 reduce-scatter.1
where the time goes:
time: 267 us; the launch traced here: 263 us
  waiting for transfers between devices  85.3 us (32%)
  blocking collectives  61.5 us (23%)
  other arithmetic  39.9 us (15%)
  local copies, waits for them, and re-layouts  32.2 us (12%)
  matrix products  29 us (11%)
  between operations  13.9 us (5%)
    unnamed x1, blocking collectives  61.5 us
    select_n x32, other arithmetic, step(): return jax.tree.map(lambda a, b: jnp.where(reached, a, b), new, before)  33.7 us
    reduce_scatter x1, waiting for transfers between devices, body(): lax.psum_scatter(jnp.dot(flat, w_out, preferred_element_type=jnp.float32)...  33.2 us
    all_gather x1, waiting for transfers between devices, entering(): everything = jax.tree.map(lambda part: lax.all_gather(part, axis), x)  27.7 us
    all_gather x1, waiting for transfers between devices, body(): lax.all_gather(activations, 'tensor', axis=0, tiled=True)  23.6 us
    unnamed x13, local copies, waits for them, and re-layouts  14.3 us
    dot_general x1, matrix products, body(): jnp.dot(lax.all_gather(activations, 'tensor', axis=0, tiled=True), weight...  8.64 us
    reshape x4, local copies, waits for them, and re-layouts, reshape_into_blocks(): array.reshape(n_blocks, BLOCK, resident_attention_heads, HEAD_DIM)  7.8 us
  transfers between devices with their start and end apart: 3, of which 3 were waited for; matrix products, arithmetic and copies ran while one was open for 8% of the time, Pallas kernels for 0%

commit v1 on v0

v1 whole, which is shorter than its diff:
```python
import functools

import jax
import jax.numpy as jnp
from jax import lax
from jax.experimental import pallas as pl
from jax.experimental.pallas import tpu as pltpu
from jax.sharding import PartitionSpec as P

HEAD_DIM = 128
BLOCK = 256
ROWS = 64
HEADS = 4
N_TENSOR = 8
N_Y = 4
IN_CHUNKS = 6
OUT_CHUNKS = 8
LAG = 2
AHEAD = 2
F32 = jnp.float32
BF16 = jnp.bfloat16


def silu(v):
    half = 0.5 * v
    return half + half * jnp.tanh(half)


def kernel(
    n_ctx, x_ref, w_ref, wo_ref, ld_ref, out_ref,
    xall, wv, w2, acc, q_s, qs_s, k_s, v_s, mask_s, eq_s, ek_s, inner_s, u_s,
    ld8, cum_s, elast_s, dsend, dec, edec,
    st1, rc1, st2, rc2, nsend, nrm, part, relay, summed, from_b, from_f,
    ag_send, ag_b, ag_f, ag_o, ag_s, own_sem, w_sem, wo_own, wo_send, wo_recv,
    dec_send, dec_recv, p1_send, p1_recv, p2_send, p2_recv, n_send, n_recv,
    rs_send, rs_relay, rs_b, rs_f, rs_sum_send,
):
    ctx = lax.axis_index("context")
    t = lax.axis_index("tensor")
    y = t // 2
    core = t % 2
    other = 1 - core
    sib = y * 2 + other
    d_model = x_ref.shape[1]
    kc = d_model // IN_CHUNKS
    nc = d_model // OUT_CHUNKS
    chunk_rows = HEADS * HEAD_DIM // n_ctx

    def remote(src, dst, send, recv, device):
        return pltpu.make_async_remote_copy(
            src_ref=src, dst_ref=dst, send_sem=send, recv_sem=recv,
            device_id=device, device_id_type=pl.DeviceIdType.MESH,
        )

    def ring(j):
        step = 1 - 2 * ((j + core) % 2)
        fwd = (y + step + N_Y) % N_Y
        bwd = (y - step + N_Y) % N_Y
        return fwd, bwd

    def in_cols(j):
        return pl.ds(pl.multiple_of(j * kc, kc), kc)

    def out_cols(j):
        return pl.ds(pl.multiple_of(j * nc, nc), nc)

    def w_copy(j):
        rows = in_cols(j)
        return pltpu.make_async_copy(w_ref.at[:, rows, :], wv.at[:, rows, :], w_sem.at[j])

    def own_copy(j):
        cols = in_cols(j)
        return pltpu.make_async_copy(x_ref.at[:, cols], xall.at[t, :, cols], own_sem.at[j])

    def send_own(j):
        cols = in_cols(j)
        fwd, bwd = ring(j)
        src, dst = x_ref.at[:, cols], xall.at[t, :, cols]
        remote(src, dst, ag_send, ag_b.at[j], {"tensor": fwd * 2 + core}).start()
        remote(src, dst, ag_send, ag_f.at[j], {"tensor": bwd * 2 + core}).start()
        remote(src, dst, ag_send, ag_s.at[j], {"tensor": sib}).start()

    def to_sibling(slot, j):
        part_ref = xall.at[slot, :, in_cols(j)]
        remote(part_ref, part_ref, ag_send, ag_s.at[j], {"tensor": sib}).start()

    def wait_slot(slot, j, sem):
        part_ref = xall.at[slot, :, in_cols(j)]
        remote(part_ref, part_ref, ag_send, sem.at[j], {"tensor": sib}).wait_recv()

    for j in range(IN_CHUNKS):
        own_copy(j).start()
        w_copy(j).start()
    wo_copy = pltpu.make_async_copy(wo_ref, w2.at[pl.ds(0, HEADS * HEAD_DIM)], wo_own)
    wo_copy.start()

    barrier = pltpu.get_barrier_semaphore()
    for peer in (((y + 1) % N_Y) * 2 + core, ((y + N_Y - 1) % N_Y) * 2 + core, sib):
        pl.semaphore_signal(
            barrier, inc=1, device_id={"tensor": peer}, device_id_type=pl.DeviceIdType.MESH
        )

    def greet(i, carry):
        pl.semaphore_signal(
            barrier, inc=1, device_id={"context": (ctx + i) % n_ctx},
            device_id_type=pl.DeviceIdType.MESH,
        )
        return carry

    lax.fori_loop(1, n_ctx, greet, 0)
    pl.semaphore_wait(barrier, 3 + n_ctx - 1)

    for j in range(AHEAD):
        send_own(j)

    ld8[0:HEADS, :] = ld_ref[:, 0:BLOCK]
    ld8[HEADS : 2 * HEADS, :] = ld_ref[:, BLOCK : 2 * BLOCK]
    cum = ld8[...]
    lane = lax.broadcasted_iota(jnp.int32, (2 * HEADS, BLOCK), 1)
    shift = 1
    while shift < BLOCK:
        cum = cum + jnp.where(lane >= shift, pltpu.roll(cum, shift, 1), 0.0)
        shift *= 2
    cum_s[...] = cum
    last = jnp.broadcast_to(cum[:, BLOCK - 1 : BLOCK], (2 * HEADS, HEAD_DIM))
    elast_s[...] = jnp.exp(last)
    both = last + pltpu.roll(last, HEADS, 0)
    dsend[...] = both
    dec[pl.ds(ctx, 1)] = both[None]

    def send_decay(i, carry):
        remote(
            dsend, dec.at[ctx], dec_send, dec_recv, {"context": (ctx + i) % n_ctx}
        ).start()
        return carry

    lax.fori_loop(1, n_ctx, send_decay, 0)

    def decay_tables(r, carry):
        row = cum_s[pl.ds(r, 1), :]
        column = jnp.transpose(jnp.broadcast_to(row, (HEAD_DIM, BLOCK)))
        end = row[:, BLOCK - 1 : BLOCK]
        eq_s[r] = jnp.exp(column).reshape(2, 2, ROWS, HEAD_DIM)
        ek_s[r] = jnp.exp(end - column)
        for half in range(2):
            at = half * HEAD_DIM
            gaps = jnp.minimum(column - row[:, at : at + HEAD_DIM], 0.0)
            i = lax.broadcasted_iota(jnp.int32, (BLOCK, HEAD_DIM), 0)
            k = lax.broadcasted_iota(jnp.int32, (BLOCK, HEAD_DIM), 1) + at
            mask_s[r, :, at : at + HEAD_DIM] = jnp.where(i >= k, jnp.exp(gaps), 0.0)
        return carry

    lax.fori_loop(0, 2 * HEADS, decay_tables, 0)
    acc[...] = jnp.zeros_like(acc)

    def forward(j):
        fwd, bwd = ring(j)
        wait_slot(bwd * 2 + core, j, ag_b)
        src = xall.at[bwd * 2 + core, :, in_cols(j)]
        remote(src, src, ag_send, ag_o.at[j], {"tensor": fwd * 2 + core}).start()
        to_sibling(bwd * 2 + core, j)
        wait_slot(fwd * 2 + core, j, ag_f)
        to_sibling(fwd * 2 + core, j)

    def opposite(j):
        slot = ((y + 2) % N_Y) * 2 + core
        wait_slot(slot, j, ag_o)
        to_sibling(slot, j)

    def finish(j):
        four = xall.at[pl.ds(0, 4), :, in_cols(j)]
        remote(four, four, ag_send, ag_s.at[j], {"tensor": sib}).wait_recv()
        own_copy(j).wait()
        w_copy(j).wait()

    def multiply(j, parts):
        rows = xall[:, :, in_cols(j)].reshape(N_TENSOR * ROWS, kc)
        for i in parts:
            acc[i] += jnp.dot(rows, wv[i, in_cols(j), :], preferred_element_type=F32)

    wo_rows = HEADS * HEAD_DIM // IN_CHUNKS // 16 * 16

    def send_w_out():
        remote(
            wo_ref, w2.at[pl.ds(HEADS * HEAD_DIM, HEADS * HEAD_DIM)],
            wo_send, wo_recv, {"tensor": sib},
        ).start()

    forward(0)

    def gather_step(j, carry):
        @pl.when(j + AHEAD - 1 < IN_CHUNKS)
        def _():
            send_own(j + AHEAD - 1)

        forward(j)
        opposite(j - 1)
        finish(j - 1)
        multiply(j - 1, (0, 1, 2))
        return carry

    send_w_out()
    lax.fori_loop(1, IN_CHUNKS, gather_step, 0)

    def decay_size():
        return remote(
            dec.at[pl.ds(0, n_ctx - 1)], dec.at[pl.ds(0, n_ctx - 1)],
            dec_send, dec_recv, {"tensor": sib},
        )

    decay_size().wait_recv()
    my_head = ctx * chunk_rows // HEAD_DIM
    for i in range(n_ctx):
        edec[i : i + 1, :] = jnp.exp(dec[i, pl.ds(my_head, 1), :])

    opposite(IN_CHUNKS - 1)
    finish(IN_CHUNKS - 1)
    multiply(IN_CHUNKS - 1, (1, 2))

    for h in range(HEADS):
        lanes = slice(h * HEAD_DIM, (h + 1) * HEAD_DIM)
        keys = silu(acc[1, :, lanes]).astype(BF16)
        values = acc[2, :, lanes].astype(BF16)
        k_s[h] = keys
        v_s[h] = values
        states = []
        for n in range(2):
            rows = slice(n * BLOCK, (n + 1) * BLOCK)
            weighted = (keys[rows].astype(F32) * ek_s[n * HEADS + h]).astype(BF16)
            states.append(
                lax.dot_general(
                    weighted, values[rows], (((0,), (0,)), ((), ())), preferred_element_type=F32
                )
            )
        u_s[h] = states[0]
        total = elast_s[HEADS + h : HEADS + h + 1, :] * states[0] + states[1]
        pieces = HEAD_DIM // chunk_rows
        st1[h * pieces : (h + 1) * pieces] = total.astype(BF16).reshape(
            pieces, chunk_rows, HEAD_DIM
        )

    def send_state(i, carry):
        to = (ctx + i) % n_ctx
        remote(st1.at[to], rc1.at[ctx], p1_send, p1_recv, {"context": to}).start()
        return carry

    lax.fori_loop(1, n_ctx, send_state, 0)
    rc1[pl.ds(ctx, 1)] = st1[pl.ds(ctx, 1)]

    multiply(IN_CHUNKS - 1, (0,))

    def attend(n):
        for h in range(HEADS):
            lanes = slice(h * HEAD_DIM, (h + 1) * HEAD_DIM)
            rows = slice(n * BLOCK, (n + 1) * BLOCK)
            queries = silu(acc[0, rows, lanes]).astype(BF16)
            weights = lax.dot_general(
                queries, k_s[h, rows, :], (((1,), (1,)), ((), ())), preferred_element_type=F32
            )
            weights = (weights * mask_s[n * HEADS + h]).astype(BF16)
            inner_s[h, 2 * n : 2 * n + 2] = jnp.dot(
                weights, v_s[h, rows, :], preferred_element_type=F32
            ).reshape(2, 2, ROWS, HEAD_DIM)
            scaled = queries.astype(F32).reshape(2, 2, ROWS, HEAD_DIM) * eq_s[n * HEADS + h]
            qs_s[h, 2 * n : 2 * n + 2] = scaled.astype(BF16)

    attend(0)

    def state_size(buffer, send, recv):
        piece = buffer.at[pl.ds(0, n_ctx - 1)]
        return remote(piece, piece, send, recv, {"tensor": sib})

    state_size(rc1, p1_send, p1_recv).wait_recv()
    running = jnp.zeros((chunk_rows, HEAD_DIM), F32)
    for i in range(n_ctx):
        st2[i] = running.astype(BF16)

        @pl.when(ctx != i)
        def _():
            remote(st2.at[i], rc2.at[ctx], p2_send, p2_recv, {"context": i}).start()

        running = running * edec[i : i + 1, :] + rc1[i].astype(F32)
    rc2[pl.ds(ctx, 1)] = st2[pl.ds(ctx, 1)]

    attend(1)

    state_size(rc2, p2_send, p2_recv).wait_recv()

    pieces = HEAD_DIM // chunk_rows

    def normalize(which, target):
        for h in range(HEADS):
            lanes = slice(h * HEAD_DIM, (h + 1) * HEAD_DIM)
            entering = rc2[h * pieces : (h + 1) * pieces].reshape(HEAD_DIM, HEAD_DIM)
            later = elast_s[h : h + 1, :] * entering.astype(F32) + u_s[h]
            for n, state in enumerate((entering, later.astype(BF16))):
                queries = qs_s[h, 2 * n : 2 * n + 2, which].reshape(2 * ROWS, HEAD_DIM)
                attended = inner_s[h, 2 * n : 2 * n + 2, which].reshape(
                    2 * ROWS, HEAD_DIM
                ) + jnp.dot(queries, state, preferred_element_type=F32)
                size = jnp.mean(attended * attended, axis=1, keepdims=True)
                normed = (attended * lax.rsqrt(size + 1e-06)).astype(BF16)
                target[2 * n : 2 * n + 2, :, lanes] = normed.reshape(2, ROWS, HEAD_DIM)

    width = HEADS * HEAD_DIM
    normalize(other, nsend)
    norm_copy = remote(
        nsend, nrm.at[:, :, pl.ds(width, width)], n_send, n_recv, {"tensor": sib}
    )
    norm_copy.start()
    normalize(core, nrm)
    wo_copy.wait()
    w2_half = w2.at[pl.ds(width, width)]
    wo_wait = remote(w2_half, w2_half, wo_send, wo_recv, {"tensor": sib})
    wo_wait.wait_recv()
    norm_copy.wait_recv()

    def project(j):
        cols = out_cols(j)
        rows = nrm[...].reshape(N_Y * ROWS, 2 * width)
        chunk = jnp.dot(rows, w2[:, cols], preferred_element_type=F32).astype(BF16)
        part[:, :, cols] = chunk.reshape(N_Y, ROWS, nc)
        fwd, bwd = ring(j)
        remote(
            part.at[(y + 2) % N_Y, :, cols], relay.at[:, cols],
            rs_send, rs_relay.at[j], {"tensor": fwd * 2 + core},
        ).start()
        remote(
            part.at[bwd, :, cols], from_f.at[:, cols],
            rs_send, rs_f.at[j], {"tensor": bwd * 2 + core},
        ).start()

    def pass_on(j):
        cols = out_cols(j)
        fwd, _ = ring(j)
        remote(
            relay.at[:, cols], relay.at[:, cols], rs_send, rs_relay.at[j], {"tensor": sib}
        ).wait_recv()
        summed[:, cols] = (
            part[pl.ds(fwd, 1), :, cols].reshape(ROWS, nc).astype(F32)
            + relay[:, cols].astype(F32)
        ).astype(BF16)
        remote(
            summed.at[:, cols], from_b.at[:, cols],
            rs_sum_send, rs_b.at[j], {"tensor": fwd * 2 + core},
        ).start()

    def finish_rows(j):
        cols = out_cols(j)
        remote(
            from_f.at[:, cols], from_f.at[:, cols], rs_send, rs_f.at[j], {"tensor": sib}
        ).wait_recv()
        remote(
            from_b.at[:, cols], from_b.at[:, cols], rs_send, rs_b.at[j], {"tensor": sib}
        ).wait_recv()
        out_ref[:, cols] = (
            part[pl.ds(y, 1), :, cols].reshape(ROWS, nc).astype(F32)
            + from_f[:, cols].astype(F32)
            + from_b[:, cols].astype(F32)
        ).astype(out_ref.dtype)

    def project_step(j, carry):
        project(j)

        @pl.when(j >= LAG)
        def _():
            pass_on(j - LAG)

        return carry

    lax.fori_loop(0, OUT_CHUNKS, project_step, 0)

    def pass_step(j, carry):
        pass_on(j)
        finish_rows(j - (OUT_CHUNKS - LAG))
        return carry

    lax.fori_loop(OUT_CHUNKS - LAG, OUT_CHUNKS, pass_step, 0)

    seven = xall.at[pl.ds(0, 7)]
    remote(seven, seven, ag_send, ag_s.at[0], {"tensor": sib}).wait_send()
    wo_wait.wait_send()
    decay_size().wait_send()
    state_size(st1, p1_send, p1_recv).wait_send()
    state_size(st2, p2_send, p2_recv).wait_send()
    norm_copy.wait_send()

    def finish_step(j, carry):
        finish_rows(j)
        return carry

    lax.fori_loop(LAG, OUT_CHUNKS, finish_step, 0)
    two = part.at[pl.ds(0, 2)]
    remote(two, two, rs_send, rs_f.at[0], {"tensor": sib}).wait_send()
    remote(summed, summed, rs_sum_send, rs_b.at[0], {"tensor": sib}).wait_send()


def body(n_ctx, activations, w_qkv, w_out, log_decay):
    rows, d_model = activations.shape
    width = HEADS * HEAD_DIM
    chunk_rows = width // n_ctx
    any_space = pl.BlockSpec(memory_space=pl.ANY)
    vmem = pl.BlockSpec(memory_space=pltpu.VMEM)
    dma = pltpu.SemaphoreType.DMA
    shard = N_TENSOR * rows
    scratch = [
        pltpu.VMEM((N_TENSOR, rows, d_model), BF16),
        pltpu.VMEM((3, d_model, width), BF16),
        pltpu.VMEM((2 * width, d_model), BF16),
        pltpu.VMEM((3, shard, width), F32),
        pltpu.VMEM((HEADS, shard, HEAD_DIM), BF16),
        pltpu.VMEM((HEADS, N_Y, 2, rows, HEAD_DIM), BF16),
        pltpu.VMEM((HEADS, shard, HEAD_DIM), BF16),
        pltpu.VMEM((HEADS, shard, HEAD_DIM), BF16),
        pltpu.VMEM((2 * HEADS, BLOCK, BLOCK), F32),
        pltpu.VMEM((2 * HEADS, 2, 2, rows, HEAD_DIM), F32),
        pltpu.VMEM((2 * HEADS, BLOCK, HEAD_DIM), F32),
        pltpu.VMEM((HEADS, N_Y, 2, rows, HEAD_DIM), F32),
        pltpu.VMEM((HEADS, HEAD_DIM, HEAD_DIM), F32),
        pltpu.VMEM((2 * HEADS, BLOCK), F32),
        pltpu.VMEM((2 * HEADS, BLOCK), F32),
        pltpu.VMEM((2 * HEADS, HEAD_DIM), F32),
        pltpu.VMEM((2 * HEADS, HEAD_DIM), F32),
        pltpu.VMEM((n_ctx, 2 * HEADS, HEAD_DIM), F32),
        pltpu.VMEM((n_ctx, HEAD_DIM), F32),
        pltpu.VMEM((n_ctx, chunk_rows, HEAD_DIM), BF16),
        pltpu.VMEM((n_ctx, chunk_rows, HEAD_DIM), BF16),
        pltpu.VMEM((n_ctx, chunk_rows, HEAD_DIM), BF16),
        pltpu.VMEM((n_ctx, chunk_rows, HEAD_DIM), BF16),
        pltpu.VMEM((N_Y, rows, width), BF16),
        pltpu.VMEM((N_Y, rows, 2 * width), BF16),
        pltpu.VMEM((N_Y, rows, d_model), BF16),
        pltpu.VMEM((rows, d_model), BF16),
        pltpu.VMEM((rows, d_model), BF16),
        pltpu.VMEM((rows, d_model), BF16),
        pltpu.VMEM((rows, d_model), BF16),
        dma,
        dma((IN_CHUNKS,)),
        dma((IN_CHUNKS,)),
        dma((IN_CHUNKS,)),
        dma((IN_CHUNKS,)),
        dma((IN_CHUNKS,)),
        dma((IN_CHUNKS,)),
        dma,
        dma,
        dma,
        dma,
        dma,
        dma,
        dma,
        dma,
        dma,
        dma,
        dma,
        dma,
        dma((OUT_CHUNKS,)),
        dma((OUT_CHUNKS,)),
        dma((OUT_CHUNKS,)),
        dma,
    ]
    return pl.pallas_call(
        functools.partial(kernel, n_ctx),
        out_shape=jax.ShapeDtypeStruct((rows, d_model), BF16),
        in_specs=[any_space, any_space, any_space, vmem],
        out_specs=vmem,
        scratch_shapes=scratch,
        compiler_params=pltpu.CompilerParams(
            collective_id=0, has_side_effects=True, vmem_limit_bytes=52 * 1024 * 1024
        ),
    )(activations, w_qkv.transpose(1, 0, 2), w_out, log_decay)


def solution(mesh):
    in_specs = (
        P(("context", "tensor"), None),
        P(None, None, "tensor"),
        P("tensor", None),
        P("tensor", "context"),
    )
    out_specs = P(("context", "tensor"), None)
    return jax.shard_map(
        functools.partial(body, mesh.shape["context"]),
        mesh=mesh, in_specs=in_specs, out_specs=out_specs, check_vma=False,
    )
```

time: 267 us -> 71.7 us (0.27); the launches traced: 263 us -> 71.5 us
  waiting for transfers between devices: 85.3 us -> 0 us
  Pallas kernels: 0 us -> 69.1 us
  blocking collectives: 61.5 us -> 0 us
  other arithmetic: 39.9 us -> 0 us
  local copies, waits for them, and re-layouts: 32.2 us -> 2.44 us
  matrix products: 29 us -> 0 us
  between operations: 13.9 us -> 0.01 us
    pallas_call x0 -> x1, Pallas kernels: none -> 69.1 us  [body(): pl.pallas_call(functools.partial(kernel, n_ctx), out_shape=jax.ShapeDtype...]
    unnamed x1 -> x0, blocking collectives: 61.5 us -> none
    all_gather x2 -> x0, waiting for transfers between devices: 51.3 us -> none  [the longest x1 27.7 us: entering(): everything = jax.tree.map(lambda part: lax.all_gather(part, axis), x)]
    select_n x32 -> x0, other arithmetic: 33.7 us -> none  [step(): return jax.tree.map(lambda a, b: jnp.where(reached, a, b), new, before)]
    reduce_scatter x1 -> x0, waiting for transfers between devices: 33.2 us -> none  [body(): lax.psum_scatter(jnp.dot(flat, w_out, preferred_element_type=jnp.float32)...]
    dot_general x9 -> x0, matrix products: 29 us -> none  [the longest x1 8.64 us: body(): jnp.dot(lax.all_gather(activations, 'tensor', axis=0, tiled=True), weight...]
    unnamed x13 -> x5, local copies, waits for them, and re-layouts: 14.3 us -> 2.44 us
    reshape x7 -> x0, local copies, waits for them, and re-layouts: 10.9 us -> none  [the longest x4 7.8 us: reshape_into_blocks(): array.reshape(n_blocks, BLOCK, resident_attention_heads, HEAD_DIM)]
  transfers between devices with their start and end apart: 3 -> 0, of which waited for: 3 -> 0; matrix products, arithmetic and copies ran while one was open for 8% -> 0% of each run, Pallas kernels for 0% -> 0%
where the time goes in v1:
time: 71.7 us; the launch traced here: 71.5 us
  Pallas kernels  69.1 us (96%)
  local copies, waits for them, and re-layouts  2.44 us (3%)
    pallas_call x1, Pallas kernels, body(): pl.pallas_call(functools.partial(kernel, n_ctx), out_shape=jax.ShapeDtype...  69.1 us
    unnamed x5, local copies, waits for them, and re-layouts  2.44 us

profile of v1, /device:TPU:1, one launch (start us, length us, event | category | flops | bytes accessed | tf_op | source)
XLA Modules:
  0.0 71.5 jit_solution(11677284315544430881)
XLA Ops:
  0.0 0.0 copy-start
  0.0 1.0 %copy-done = bf16[64,3072]{1,0:T(8,128)(2,1)S(1)} copy-done((bf16[64,3072]{1,0:T(8,128)(2,1)S(1)}, bf16[64,3072]{1,0:T(8,128)(2,1)}, u32[]{:S(2)}) %copy-start) | copy-done | bytes 393240
  1.0 0.0 copy-start.1
  1.0 0.7 copy-done.1
  1.7 69.1 %shard_map.46 = bf16[64,3072]{1,0:T(8,128)(2,1)S(1)} custom-call(bf16[64,3072]{1,0:T(8,128)(2,1)S(1)} %copy-done, bf16[3,3072,512]{2,1,0:T(8,128)(2,1)} %bitcast.1, bf16[512,3072]{1,0:T(8,128)(2,1)} %wo_ref.1, f32[4,512]{1,0:T(4,128)S(1)} %copy-done.1), custom_call_target="tpu_custom_call" | custom-call | tf_op jit(solution)/shard_map/pallas_call | solution.py:461
  70.8 0.7 %copy.6 = bf16[64,3072]{1,0:T(8,128)(2,1)} copy(bf16[64,3072]{1,0:T(8,128)(2,1)S(1)} %shard_map.46) | data formatting | bytes 786432
Async XLA Ops:
  0.0 1.0 %copy-start = (bf16[64,3072]{1,0:T(8,128)(2,1)S(1)}, bf16[64,3072]{1,0:T(8,128)(2,1)}, u32[]{:S(2)}) copy-start(bf16[64,3072]{1,0:T(8,128)(2,1)} %x_ref.1) | copy-start | bytes 1179652
  1.0 0.7 copy-start.1

commit v2 on v1

--- a/solution.py
+++ b/solution.py
@@ -13,10 +13,13 @@
 HEADS = 4
 N_TENSOR = 8
 N_Y = 4
-IN_CHUNKS = 6
-OUT_CHUNKS = 8
-LAG = 2
+IN_CHUNKS = (512,) * 6
+N_IN = len(IN_CHUNKS)
+OUT_CHUNKS = 6
+LAG = 3
 AHEAD = 2
+OPP_LAG = 2
+MUL_LAG = 3
 F32 = jnp.float32
 BF16 = jnp.bfloat16
 
@@ -29,11 +32,11 @@
 def kernel(
     n_ctx, x_ref, w_ref, wo_ref, ld_ref, out_ref,
     xall, wv, w2, acc, q_s, qs_s, k_s, v_s, mask_s, eq_s, ek_s, inner_s, u_s,
-    ld8, cum_s, elast_s, dsend, dec, edec,
+    ld4, ld8, cum_s, elast_s, dsend, dec, edec,
     st1, rc1, st2, rc2, nsend, nrm, part, relay, summed, from_b, from_f,
     ag_send, ag_b, ag_f, ag_o, ag_s, own_sem, w_sem, wo_own, wo_send, wo_recv,
     dec_send, dec_recv, p1_send, p1_recv, p2_send, p2_recv, n_send, n_recv,
-    rs_send, rs_relay, rs_b, rs_f, rs_sum_send,
+    rs_send, rs_relay, rs_b, rs_f, rs_sum_send, ld_sem,
 ):
     ctx = lax.axis_index("context")
     t = lax.axis_index("tensor")
@@ -42,9 +45,22 @@
     other = 1 - core
     sib = y * 2 + other
     d_model = x_ref.shape[1]
-    kc = d_model // IN_CHUNKS
     nc = d_model // OUT_CHUNKS
     chunk_rows = HEADS * HEAD_DIM // n_ctx
+
+    n_x = 4
+    n_z = n_ctx // n_x
+
+    def hops(dz, dx):
+        return min(dz, n_z - dz) + min(dx, n_x - dx)
+
+    others = sorted(
+        ((dz, dx) for dz in range(n_z) for dx in range(n_x) if dz or dx),
+        key=lambda d: -hops(*d),
+    )
+    peers = [
+        (ctx // n_x + dz) % n_z * n_x + (ctx % n_x + dx) % n_x for dz, dx in others
+    ]
 
     def remote(src, dst, send, recv, device):
         return pltpu.make_async_remote_copy(
@@ -59,7 +75,7 @@
         return fwd, bwd
 
     def in_cols(j):
-        return pl.ds(pl.multiple_of(j * kc, kc), kc)
+        return pl.ds(sum(IN_CHUNKS[:j]), IN_CHUNKS[j])
 
     def out_cols(j):
         return pl.ds(pl.multiple_of(j * nc, nc), nc)
@@ -88,7 +104,9 @@
         part_ref = xall.at[slot, :, in_cols(j)]
         remote(part_ref, part_ref, ag_send, sem.at[j], {"tensor": sib}).wait_recv()
 
-    for j in range(IN_CHUNKS):
+    ld_copy = pltpu.make_async_copy(ld_ref, ld4, ld_sem)
+    ld_copy.start()
+    for j in range(N_IN):
         own_copy(j).start()
         w_copy(j).start()
     wo_copy = pltpu.make_async_copy(wo_ref, w2.at[pl.ds(0, HEADS * HEAD_DIM)], wo_own)
@@ -113,8 +131,9 @@
     for j in range(AHEAD):
         send_own(j)
 
-    ld8[0:HEADS, :] = ld_ref[:, 0:BLOCK]
-    ld8[HEADS : 2 * HEADS, :] = ld_ref[:, BLOCK : 2 * BLOCK]
+    ld_copy.wait()
+    ld8[0:HEADS, :] = ld4[:, 0:BLOCK]
+    ld8[HEADS : 2 * HEADS, :] = ld4[:, BLOCK : 2 * BLOCK]
     cum = ld8[...]
     lane = lax.broadcasted_iota(jnp.int32, (2 * HEADS, BLOCK), 1)
     shift = 1
@@ -136,7 +155,7 @@
 
     lax.fori_loop(1, n_ctx, send_decay, 0)
 
-    def decay_tables(r, carry):
+    def decay_tables(r):
         row = cum_s[pl.ds(r, 1), :]
         column = jnp.transpose(jnp.broadcast_to(row, (HEAD_DIM, BLOCK)))
         end = row[:, BLOCK - 1 : BLOCK]
@@ -148,9 +167,7 @@
             i = lax.broadcasted_iota(jnp.int32, (BLOCK, HEAD_DIM), 0)
             k = lax.broadcasted_iota(jnp.int32, (BLOCK, HEAD_DIM), 1) + at
             mask_s[r, :, at : at + HEAD_DIM] = jnp.where(i >= k, jnp.exp(gaps), 0.0)
-        return carry
-
-    lax.fori_loop(0, 2 * HEADS, decay_tables, 0)
+
     acc[...] = jnp.zeros_like(acc)
 
     def forward(j):
@@ -174,33 +191,22 @@
         w_copy(j).wait()
 
     def multiply(j, parts):
-        rows = xall[:, :, in_cols(j)].reshape(N_TENSOR * ROWS, kc)
+        rows = xall[:, :, in_cols(j)].reshape(N_TENSOR * ROWS, IN_CHUNKS[j])
         for i in parts:
             acc[i] += jnp.dot(rows, wv[i, in_cols(j), :], preferred_element_type=F32)
 
-    wo_rows = HEADS * HEAD_DIM // IN_CHUNKS // 16 * 16
-
-    def send_w_out():
-        remote(
-            wo_ref, w2.at[pl.ds(HEADS * HEAD_DIM, HEADS * HEAD_DIM)],
-            wo_send, wo_recv, {"tensor": sib},
-        ).start()
-
-    forward(0)
-
-    def gather_step(j, carry):
-        @pl.when(j + AHEAD - 1 < IN_CHUNKS)
-        def _():
-            send_own(j + AHEAD - 1)
-
-        forward(j)
-        opposite(j - 1)
-        finish(j - 1)
-        multiply(j - 1, (0, 1, 2))
-        return carry
-
-    send_w_out()
-    lax.fori_loop(1, IN_CHUNKS, gather_step, 0)
+    for j in range(N_IN + MUL_LAG - 1):
+        if AHEAD <= j + AHEAD < N_IN:
+            send_own(j + AHEAD)
+        if j < N_IN:
+            forward(j)
+        if j < 2 * HEADS:
+            decay_tables(j)
+        if 0 <= j - OPP_LAG < N_IN:
+            opposite(j - OPP_LAG)
+        if 0 <= j - MUL_LAG < N_IN - 1:
+            finish(j - MUL_LAG)
+            multiply(j - MUL_LAG, (0, 1, 2))
 
     def decay_size():
         return remote(
@@ -213,9 +219,12 @@
     for i in range(n_ctx):
         edec[i : i + 1, :] = jnp.exp(dec[i, pl.ds(my_head, 1), :])
 
-    opposite(IN_CHUNKS - 1)
-    finish(IN_CHUNKS - 1)
-    multiply(IN_CHUNKS - 1, (1, 2))
+    finish(N_IN - 1)
+    multiply(N_IN - 1, (1, 2))
+    remote(
+        wo_ref, w2.at[pl.ds(HEADS * HEAD_DIM, HEADS * HEAD_DIM)],
+        wo_send, wo_recv, {"tensor": sib},
+    ).start()
 
     for h in range(HEADS):
         lanes = slice(h * HEAD_DIM, (h + 1) * HEAD_DIM)
@@ -239,15 +248,11 @@
             pieces, chunk_rows, HEAD_DIM
         )
 
-    def send_state(i, carry):
-        to = (ctx + i) % n_ctx
+    for to in peers:
         remote(st1.at[to], rc1.at[ctx], p1_send, p1_recv, {"context": to}).start()
-        return carry
-
-    lax.fori_loop(1, n_ctx, send_state, 0)
     rc1[pl.ds(ctx, 1)] = st1[pl.ds(ctx, 1)]
 
-    multiply(IN_CHUNKS - 1, (0,))
+    multiply(N_IN - 1, (0,))
 
     def attend(n):
         for h in range(HEADS):
@@ -274,12 +279,9 @@
     running = jnp.zeros((chunk_rows, HEAD_DIM), F32)
     for i in range(n_ctx):
         st2[i] = running.astype(BF16)
-
-        @pl.when(ctx != i)
-        def _():
-            remote(st2.at[i], rc2.at[ctx], p2_send, p2_recv, {"context": i}).start()
-
         running = running * edec[i : i + 1, :] + rc1[i].astype(F32)
+    for to in peers:
+        remote(st2.at[to], rc2.at[ctx], p2_send, p2_recv, {"context": to}).start()
     rc2[pl.ds(ctx, 1)] = st2[pl.ds(ctx, 1)]
 
     attend(1)
@@ -399,7 +401,7 @@
     rows, d_model = activations.shape
     width = HEADS * HEAD_DIM
     chunk_rows = width // n_ctx
-    any_space = pl.BlockSpec(memory_space=pl.ANY)
+    hbm = pl.BlockSpec(memory_space=pltpu.HBM)
     vmem = pl.BlockSpec(memory_space=pltpu.VMEM)
     dma = pltpu.SemaphoreType.DMA
     shard = N_TENSOR * rows
@@ -417,6 +419,7 @@
         pltpu.VMEM((2 * HEADS, BLOCK, HEAD_DIM), F32),
         pltpu.VMEM((HEADS, N_Y, 2, rows, HEAD_DIM), F32),
         pltpu.VMEM((HEADS, HEAD_DIM, HEAD_DIM), F32),
+        pltpu.VMEM((HEADS, 2 * BLOCK), F32),
         pltpu.VMEM((2 * HEADS, BLOCK), F32),
         pltpu.VMEM((2 * HEADS, BLOCK), F32),
         pltpu.VMEM((2 * HEADS, HEAD_DIM), F32),
@@ -435,12 +438,12 @@
         pltpu.VMEM((rows, d_model), BF16),
         pltpu.VMEM((rows, d_model), BF16),
         dma,
-        dma((IN_CHUNKS,)),
-        dma((IN_CHUNKS,)),
-        dma((IN_CHUNKS,)),
-        dma((IN_CHUNKS,)),
-        dma((IN_CHUNKS,)),
-        dma((IN_CHUNKS,)),
+        dma((N_IN,)),
+        dma((N_IN,)),
+        dma((N_IN,)),
+        dma((N_IN,)),
+        dma((N_IN,)),
+        dma((N_IN,)),
         dma,
         dma,
         dma,
@@ -456,18 +459,22 @@
         dma((OUT_CHUNKS,)),
         dma((OUT_CHUNKS,)),
         dma((OUT_CHUNKS,)),
+        dma,
         dma,
     ]
     return pl.pallas_call(
         functools.partial(kernel, n_ctx),
         out_shape=jax.ShapeDtypeStruct((rows, d_model), BF16),
-        in_specs=[any_space, any_space, any_space, vmem],
+        in_specs=[hbm, hbm, hbm, hbm],
         out_specs=vmem,
         scratch_shapes=scratch,
         compiler_params=pltpu.CompilerParams(
             collective_id=0, has_side_effects=True, vmem_limit_bytes=52 * 1024 * 1024
         ),
-    )(activations, w_qkv.transpose(1, 0, 2), w_out, log_decay)
+    )(*(
+        pltpu.with_memory_space_constraint(array, pltpu.HBM)
+        for array in (activations, w_qkv.transpose(1, 0, 2), w_out, log_decay)
+    ))
 
 
 def solution(mesh):

time: 71.7 us -> 62.5 us (0.87)
  Pallas kernels: 69.1 us -> 61.6 us
  local copies, waits for them, and re-layouts: 2.44 us -> 0.75 us
    pallas_call x1, Pallas kernels: 69.1 us -> 61.6 us  [body(): pl.pallas_call(functools.partial(kernel, n_ctx), out_shape=jax.ShapeDtype...]
    unnamed x5 -> x1, local copies, waits for them, and re-layouts: 2.44 us -> 0.75 us
where the time goes in v2:
time: 62.5 us; the launch traced here: 62.4 us
  Pallas kernels  61.6 us (99%)
  local copies, waits for them, and re-layouts  0.75 us (1%)
    pallas_call x1, Pallas kernels, body(): pl.pallas_call(functools.partial(kernel, n_ctx), out_shape=jax.ShapeDtype...  61.6 us

profile of v2, /device:TPU:1, one launch (start us, length us, event | category | flops | bytes accessed | tf_op | source)
XLA Modules:
  0.0 62.4 jit_solution(8655170850649257330)
XLA Ops:
  0.0 61.6 %shard_map.46 = bf16[64,3072]{1,0:T(8,128)(2,1)S(1)} custom-call(bf16[64,3072]{1,0:T(8,128)(2,1)} %x_ref.1, bf16[3,3072,512]{2,1,0:T(8,128)(2,1)} %bitcast.1, bf16[512,3072]{1,0:T(8,128)(2,1)} %wo_ref.1, f32[4,512]{1,0:T(4,128)} %ld_ref.1), custom_call_target="tpu_custom_call" | custom-call | tf_op jit(solution)/shard_map/pallas_call | solution.py:465
  61.7 0.7 %copy.6 = bf16[64,3072]{1,0:T(8,128)(2,1)} copy(bf16[64,3072]{1,0:T(8,128)(2,1)S(1)} %shard_map.46) | data formatting | bytes 786432

commit v3 on v2

--- a/solution.py
+++ b/solution.py
@@ -17,9 +17,8 @@
 N_IN = len(IN_CHUNKS)
 OUT_CHUNKS = 6
 LAG = 3
-AHEAD = 2
-OPP_LAG = 2
-MUL_LAG = 3
+EARLY = 2
+OWN, UP, DOWN, OPPOSITE = range(N_Y)
 F32 = jnp.float32
 BF16 = jnp.bfloat16
 
@@ -31,10 +30,10 @@
 
 def kernel(
     n_ctx, x_ref, w_ref, wo_ref, ld_ref, out_ref,
-    xall, wv, w2, acc, q_s, qs_s, k_s, v_s, mask_s, eq_s, ek_s, inner_s, u_s,
+    xall, wv, w2, acc, qs_s, k_s, v_s, mask_s, eq_s, ek_s, inner_s, u_s,
     ld4, ld8, cum_s, elast_s, dsend, dec, edec,
     st1, rc1, st2, rc2, nsend, nrm, part, relay, summed, from_b, from_f,
-    ag_send, ag_b, ag_f, ag_o, ag_s, own_sem, w_sem, wo_own, wo_send, wo_recv,
+    ag_send, ag_up, ag_down, ag_o, ag_s, ag_so, own_sem, w_sem, wo_own, wo_send, wo_recv,
     dec_send, dec_recv, p1_send, p1_recv, p2_send, p2_recv, n_send, n_recv,
     rs_send, rs_relay, rs_b, rs_f, rs_sum_send, ld_sem,
 ):
@@ -86,23 +85,71 @@
 
     def own_copy(j):
         cols = in_cols(j)
-        return pltpu.make_async_copy(x_ref.at[:, cols], xall.at[t, :, cols], own_sem.at[j])
+        return pltpu.make_async_copy(x_ref.at[:, cols], xall.at[OWN, core, :, cols], own_sem.at[j])
+
+    up, down = (y + 1) % N_Y * 2, (y + N_Y - 1) % N_Y * 2
 
     def send_own(j):
         cols = in_cols(j)
-        fwd, bwd = ring(j)
-        src, dst = x_ref.at[:, cols], xall.at[t, :, cols]
-        remote(src, dst, ag_send, ag_b.at[j], {"tensor": fwd * 2 + core}).start()
-        remote(src, dst, ag_send, ag_f.at[j], {"tensor": bwd * 2 + core}).start()
-        remote(src, dst, ag_send, ag_s.at[j], {"tensor": sib}).start()
-
-    def to_sibling(slot, j):
-        part_ref = xall.at[slot, :, in_cols(j)]
-        remote(part_ref, part_ref, ag_send, ag_s.at[j], {"tensor": sib}).start()
-
-    def wait_slot(slot, j, sem):
-        part_ref = xall.at[slot, :, in_cols(j)]
-        remote(part_ref, part_ref, ag_send, sem.at[j], {"tensor": sib}).wait_recv()
+        src = xall.at[OWN, core, :, cols]
+        own_copy(j).wait()
+        remote(
+            src, xall.at[DOWN, core, :, cols], ag_send, ag_down.at[j], {"tensor": up + core}
+        ).start()
+        remote(
+            src, xall.at[UP, core, :, cols], ag_send, ag_up.at[j], {"tensor": down + core}
+        ).start()
+        remote(src, src, ag_send, ag_s.at[j], {"tensor": sib}).start()
+
+    def arrived(ref, sem):
+        remote(ref, ref, ag_send, sem, {"tensor": sib}).wait_recv()
+
+    def pass_near(j):
+        cols = in_cols(j)
+        arrived(xall.at[DOWN, core, :, cols], ag_down.at[j])
+        arrived(xall.at[UP, core, :, cols], ag_up.at[j])
+        upward = (j + core) % 2
+        chip = (y + 2 * upward + N_Y - 1) % N_Y * 2
+        src = xall.at[UP + upward, core, :, cols]
+        dst = xall.at[OPPOSITE, core, :, cols]
+        remote(src, dst, ag_send, ag_o.at[j], {"tensor": chip + core}).start()
+        if j == N_IN - 1:
+            remote(src, dst, ag_send, ag_so.at[j], {"tensor": chip + other}).start()
+        near = xall.at[pl.ds(UP, 2), core, :, cols]
+        remote(near, near, ag_send, ag_s.at[j], {"tensor": sib}).start()
+
+    def pass_opposite(j):
+        ref = xall.at[OPPOSITE, core, :, in_cols(j)]
+        arrived(ref, ag_o.at[j])
+        if j < N_IN - 1:
+            remote(ref, ref, ag_send, ag_so.at[j], {"tensor": sib}).start()
+
+    def multiply(j, slots, parts):
+        first, count = slots
+        rows = slice(first * 2 * ROWS, (first + count) * 2 * ROWS)
+        values = xall[first : first + count, :, :, in_cols(j)].reshape(
+            count * 2 * ROWS, IN_CHUNKS[j]
+        )
+        for i in parts:
+            product = jnp.dot(values, wv[i, in_cols(j), :], preferred_element_type=F32)
+            acc[i, rows] = product if j == 0 else acc[i, rows] + product
+
+    def multiply_near(j):
+        w_copy(j).wait()
+        arrived(xall.at[pl.ds(OWN, 3), other, :, in_cols(j)], ag_s.at[j])
+        multiply(j, (OWN, 3), (0, 1, 2))
+
+    def multiply_opposite(j):
+        arrived(xall.at[OPPOSITE, other, :, in_cols(j)], ag_so.at[j])
+        multiply(j, (OPPOSITE, 1), (1, 2))
+
+    def rows_of(i, chip, lanes):
+        ahead = (chip - y + N_Y) % N_Y
+        slot = ahead + ahead // 2 * (5 - 2 * ahead)
+        return acc[i, pl.ds(pl.multiple_of(slot * 2 * ROWS, 2 * ROWS), 2 * ROWS), lanes]
+
+    def block_of(i, n, lanes):
+        return jnp.concatenate([rows_of(i, 2 * n, lanes), rows_of(i, 2 * n + 1, lanes)], axis=0)
 
     ld_copy = pltpu.make_async_copy(ld_ref, ld4, ld_sem)
     ld_copy.start()
@@ -113,7 +160,7 @@
     wo_copy.start()
 
     barrier = pltpu.get_barrier_semaphore()
-    for peer in (((y + 1) % N_Y) * 2 + core, ((y + N_Y - 1) % N_Y) * 2 + core, sib):
+    for peer in (up + core, down + core, sib, up + other, down + other):
         pl.semaphore_signal(
             barrier, inc=1, device_id={"tensor": peer}, device_id_type=pl.DeviceIdType.MESH
         )
@@ -126,9 +173,9 @@
         return carry
 
     lax.fori_loop(1, n_ctx, greet, 0)
-    pl.semaphore_wait(barrier, 3 + n_ctx - 1)
-
-    for j in range(AHEAD):
+    pl.semaphore_wait(barrier, 5 + n_ctx - 1)
+
+    for j in range(N_IN):
         send_own(j)
 
     ld_copy.wait()
@@ -168,45 +215,17 @@
             k = lax.broadcasted_iota(jnp.int32, (BLOCK, HEAD_DIM), 1) + at
             mask_s[r, :, at : at + HEAD_DIM] = jnp.where(i >= k, jnp.exp(gaps), 0.0)
 
-    acc[...] = jnp.zeros_like(acc)
-
-    def forward(j):
-        fwd, bwd = ring(j)
-        wait_slot(bwd * 2 + core, j, ag_b)
-        src = xall.at[bwd * 2 + core, :, in_cols(j)]
-        remote(src, src, ag_send, ag_o.at[j], {"tensor": fwd * 2 + core}).start()
-        to_sibling(bwd * 2 + core, j)
-        wait_slot(fwd * 2 + core, j, ag_f)
-        to_sibling(fwd * 2 + core, j)
-
-    def opposite(j):
-        slot = ((y + 2) % N_Y) * 2 + core
-        wait_slot(slot, j, ag_o)
-        to_sibling(slot, j)
-
-    def finish(j):
-        four = xall.at[pl.ds(0, 4), :, in_cols(j)]
-        remote(four, four, ag_send, ag_s.at[j], {"tensor": sib}).wait_recv()
-        own_copy(j).wait()
-        w_copy(j).wait()
-
-    def multiply(j, parts):
-        rows = xall[:, :, in_cols(j)].reshape(N_TENSOR * ROWS, IN_CHUNKS[j])
-        for i in parts:
-            acc[i] += jnp.dot(rows, wv[i, in_cols(j), :], preferred_element_type=F32)
-
-    for j in range(N_IN + MUL_LAG - 1):
-        if AHEAD <= j + AHEAD < N_IN:
-            send_own(j + AHEAD)
+    for j in range(N_IN + 1):
         if j < N_IN:
-            forward(j)
-        if j < 2 * HEADS:
-            decay_tables(j)
-        if 0 <= j - OPP_LAG < N_IN:
-            opposite(j - OPP_LAG)
-        if 0 <= j - MUL_LAG < N_IN - 1:
-            finish(j - MUL_LAG)
-            multiply(j - MUL_LAG, (0, 1, 2))
+            pass_near(j)
+        for r in range(2 * HEADS):
+            if r * (N_IN + 1) // (2 * HEADS) == j:
+                decay_tables(r)
+        if j == N_IN:
+            for k in range(EARLY):
+                pass_opposite(k)
+        if j > 0:
+            multiply_near(j - 1)
 
     def decay_size():
         return remote(
@@ -219,8 +238,10 @@
     for i in range(n_ctx):
         edec[i : i + 1, :] = jnp.exp(dec[i, pl.ds(my_head, 1), :])
 
-    finish(N_IN - 1)
-    multiply(N_IN - 1, (1, 2))
+    for j in range(EARLY, N_IN + EARLY):
+        if j < N_IN:
+            pass_opposite(j)
+        multiply_opposite(j - EARLY)
     remote(
         wo_ref, w2.at[pl.ds(HEADS * HEAD_DIM, HEADS * HEAD_DIM)],
         wo_send, wo_recv, {"tensor": sib},
@@ -228,17 +249,17 @@
 
     for h in range(HEADS):
         lanes = slice(h * HEAD_DIM, (h + 1) * HEAD_DIM)
-        keys = silu(acc[1, :, lanes]).astype(BF16)
-        values = acc[2, :, lanes].astype(BF16)
-        k_s[h] = keys
-        v_s[h] = values
         states = []
         for n in range(2):
             rows = slice(n * BLOCK, (n + 1) * BLOCK)
-            weighted = (keys[rows].astype(F32) * ek_s[n * HEADS + h]).astype(BF16)
+            keys = silu(block_of(1, n, lanes)).astype(BF16)
+            values = block_of(2, n, lanes).astype(BF16)
+            k_s[h, rows] = keys
+            v_s[h, rows] = values
+            weighted = (keys.astype(F32) * ek_s[n * HEADS + h]).astype(BF16)
             states.append(
                 lax.dot_general(
-                    weighted, values[rows], (((0,), (0,)), ((), ())), preferred_element_type=F32
+                    weighted, values, (((0,), (0,)), ((), ())), preferred_element_type=F32
                 )
             )
         u_s[h] = states[0]
@@ -252,13 +273,14 @@
         remote(st1.at[to], rc1.at[ctx], p1_send, p1_recv, {"context": to}).start()
     rc1[pl.ds(ctx, 1)] = st1[pl.ds(ctx, 1)]
 
-    multiply(N_IN - 1, (0,))
+    for j in range(N_IN):
+        multiply(j, (OPPOSITE, 1), (0,))
 
     def attend(n):
         for h in range(HEADS):
             lanes = slice(h * HEAD_DIM, (h + 1) * HEAD_DIM)
             rows = slice(n * BLOCK, (n + 1) * BLOCK)
-            queries = silu(acc[0, rows, lanes]).astype(BF16)
+            queries = silu(block_of(0, n, lanes)).astype(BF16)
             weights = lax.dot_general(
                 queries, k_s[h, rows, :], (((1,), (1,)), ((), ())), preferred_element_type=F32
             )
@@ -379,7 +401,7 @@
 
     lax.fori_loop(OUT_CHUNKS - LAG, OUT_CHUNKS, pass_step, 0)
 
-    seven = xall.at[pl.ds(0, 7)]
+    seven = w2.at[pl.ds(0, 7 * ROWS)]
     remote(seven, seven, ag_send, ag_s.at[0], {"tensor": sib}).wait_send()
     wo_wait.wait_send()
     decay_size().wait_send()
@@ -406,11 +428,10 @@
     dma = pltpu.SemaphoreType.DMA
     shard = N_TENSOR * rows
     scratch = [
-        pltpu.VMEM((N_TENSOR, rows, d_model), BF16),
+        pltpu.VMEM((N_Y, 2, rows, d_model), BF16),
         pltpu.VMEM((3, d_model, width), BF16),
         pltpu.VMEM((2 * width, d_model), BF16),
         pltpu.VMEM((3, shard, width), F32),
-        pltpu.VMEM((HEADS, shard, HEAD_DIM), BF16),
         pltpu.VMEM((HEADS, N_Y, 2, rows, HEAD_DIM), BF16),
         pltpu.VMEM((HEADS, shard, HEAD_DIM), BF16),
         pltpu.VMEM((HEADS, shard, HEAD_DIM), BF16),
@@ -444,6 +465,7 @@
         dma((N_IN,)),
         dma((N_IN,)),
         dma((N_IN,)),
+        dma((N_IN,)),
         dma,
         dma,
         dma,

time: 62.5 us -> 60.7 us (0.971)
  Pallas kernels: 61.6 us -> 59.8 us
    pallas_call x1, Pallas kernels: 61.6 us -> 59.8 us  [body(): pl.pallas_call(functools.partial(kernel, n_ctx), out_shape=jax.ShapeDtype...]
where the time goes in v3:
time: 60.7 us; the launch traced here: 60.6 us
  Pallas kernels  59.8 us (99%)
  local copies, waits for them, and re-layouts  0.75 us (1%)
    pallas_call x1, Pallas kernels, body(): pl.pallas_call(functools.partial(kernel, n_ctx), out_shape=jax.ShapeDtype...  59.8 us

profile of v3, /device:TPU:1, one launch (start us, length us, event | category | flops | bytes accessed | tf_op | source)
XLA Modules:
  0.0 60.6 jit_solution(3385178584770174449)
XLA Ops:
  0.0 59.8 %shard_map.46 = bf16[64,3072]{1,0:T(8,128)(2,1)S(1)} custom-call(bf16[64,3072]{1,0:T(8,128)(2,1)} %x_ref.1, bf16[3,3072,512]{2,1,0:T(8,128)(2,1)} %bitcast.1, bf16[512,3072]{1,0:T(8,128)(2,1)} %wo_ref.1, f32[4,512]{1,0:T(4,128)} %ld_ref.1), custom_call_target="tpu_custom_call" | custom-call | tf_op jit(solution)/shard_map/pallas_call | solution.py:487
  59.9 0.7 %copy.6 = bf16[64,3072]{1,0:T(8,128)(2,1)} copy(bf16[64,3072]{1,0:T(8,128)(2,1)S(1)} %shard_map.46) | data formatting | bytes 786432

commit v4 on v3

--- a/solution.py
+++ b/solution.py
@@ -28,14 +28,20 @@
     return half + half * jnp.tanh(half)
 
 
+def split(n_ctx):
+    n_x = 4 if n_ctx > 8 else 2
+    n_half = n_ctx // 2
+    return n_x, n_ctx // n_x, n_half, HEADS * HEAD_DIM // n_half
+
+
 def kernel(
     n_ctx, x_ref, w_ref, wo_ref, ld_ref, out_ref,
     xall, wv, w2, acc, qs_s, k_s, v_s, mask_s, eq_s, ek_s, inner_s, u_s,
     ld4, ld8, cum_s, elast_s, dsend, dec, edec,
-    st1, rc1, st2, rc2, nsend, nrm, part, relay, summed, from_b, from_f,
+    st1, rc1, st2, rc2, before, after, nsend, nrm, part, relay, summed, from_b, from_f,
     ag_send, ag_up, ag_down, ag_o, ag_s, ag_so, own_sem, w_sem, wo_own, wo_send, wo_recv,
     dec_send, dec_recv, p1_send, p1_recv, p2_send, p2_recv, n_send, n_recv,
-    rs_send, rs_relay, rs_b, rs_f, rs_sum_send, ld_sem,
+    rs_send, rs_relay, rs_b, rs_f, rs_sum_send, ld_sem, half_send, half_recv, ready,
 ):
     ctx = lax.axis_index("context")
     t = lax.axis_index("tensor")
@@ -45,20 +51,25 @@
     sib = y * 2 + other
     d_model = x_ref.shape[1]
     nc = d_model // OUT_CHUNKS
-    chunk_rows = HEADS * HEAD_DIM // n_ctx
-
-    n_x = 4
-    n_z = n_ctx // n_x
-
-    def hops(dz, dx):
-        return min(dz, n_z - dz) + min(dx, n_x - dx)
+
+    n_x, n_z, n_half, chunk_rows = split(n_ctx)
+    half_z = n_z // 2
+    half, place = ctx // n_half, ctx % n_half
+    first = half * n_half
+    partner = (n_z - 1 - ctx // n_x) * n_x + ctx % n_x
+
+    def piece_of(at):
+        z = at // n_x
+        return (z + half * (half_z - 1 - 2 * z)) * n_x + at % n_x
+
+    piece = piece_of(place)
 
     others = sorted(
-        ((dz, dx) for dz in range(n_z) for dx in range(n_x) if dz or dx),
-        key=lambda d: -hops(*d),
+        ((dz, dx) for dz in range(half_z) for dx in range(n_x) if dz or dx),
+        key=lambda d: -(2 * min(d[0], 1) + min(d[1], n_x - d[1])),
     )
     peers = [
-        (ctx // n_x + dz) % n_z * n_x + (ctx % n_x + dx) % n_x for dz, dx in others
+        (place // n_x + dz) % half_z * n_x + (place % n_x + dx) % n_x for dz, dx in others
     ]
 
     def remote(src, dst, send, recv, device):
@@ -165,18 +176,32 @@
             barrier, inc=1, device_id={"tensor": peer}, device_id_type=pl.DeviceIdType.MESH
         )
 
-    def greet(i, carry):
+    for to in peers:
         pl.semaphore_signal(
-            barrier, inc=1, device_id={"context": (ctx + i) % n_ctx},
+            barrier, inc=1, device_id={"context": first + to},
             device_id_type=pl.DeviceIdType.MESH,
         )
-        return carry
-
-    lax.fori_loop(1, n_ctx, greet, 0)
-    pl.semaphore_wait(barrier, 5 + n_ctx - 1)
+
+    @pl.when(half == 0)
+    def _():
+        pl.semaphore_signal(
+            barrier, inc=1, device_id={"context": partner}, device_id_type=pl.DeviceIdType.MESH
+        )
+
+    pl.semaphore_wait(barrier, 5 + n_half - 1 + half)
 
     for j in range(N_IN):
         send_own(j)
+
+    @pl.when(half == 1)
+    def _():
+        pl.semaphore_signal(
+            ready, inc=1, device_id={"context": partner}, device_id_type=pl.DeviceIdType.MESH
+        )
+
+    @pl.when(half == 0)
+    def _():
+        before[...] = jnp.zeros_like(before)
 
     ld_copy.wait()
     ld8[0:HEADS, :] = ld4[:, 0:BLOCK]
@@ -192,15 +217,10 @@
     elast_s[...] = jnp.exp(last)
     both = last + pltpu.roll(last, HEADS, 0)
     dsend[...] = both
-    dec[pl.ds(ctx, 1)] = both[None]
-
-    def send_decay(i, carry):
-        remote(
-            dsend, dec.at[ctx], dec_send, dec_recv, {"context": (ctx + i) % n_ctx}
-        ).start()
-        return carry
-
-    lax.fori_loop(1, n_ctx, send_decay, 0)
+    dec[pl.ds(place, 1)] = both[None]
+
+    for to in peers:
+        remote(dsend, dec.at[place], dec_send, dec_recv, {"context": first + to}).start()
 
     def decay_tables(r):
         row = cum_s[pl.ds(r, 1), :]
@@ -229,13 +249,13 @@
 
     def decay_size():
         return remote(
-            dec.at[pl.ds(0, n_ctx - 1)], dec.at[pl.ds(0, n_ctx - 1)],
+            dec.at[pl.ds(0, n_half - 1)], dec.at[pl.ds(0, n_half - 1)],
             dec_send, dec_recv, {"tensor": sib},
         )
 
     decay_size().wait_recv()
-    my_head = ctx * chunk_rows // HEAD_DIM
-    for i in range(n_ctx):
+    my_head = piece * chunk_rows // HEAD_DIM
+    for i in range(n_half):
         edec[i : i + 1, :] = jnp.exp(dec[i, pl.ds(my_head, 1), :])
 
     for j in range(EARLY, N_IN + EARLY):
@@ -270,8 +290,10 @@
         )
 
     for to in peers:
-        remote(st1.at[to], rc1.at[ctx], p1_send, p1_recv, {"context": to}).start()
-    rc1[pl.ds(ctx, 1)] = st1[pl.ds(ctx, 1)]
+        remote(
+            st1.at[piece_of(to)], rc1.at[place], p1_send, p1_recv, {"context": first + to}
+        ).start()
+    rc1[pl.ds(place, 1)] = st1[pl.ds(piece, 1)]
 
     for j in range(N_IN):
         multiply(j, (OPPOSITE, 1), (0,))
@@ -294,17 +316,32 @@
     attend(0)
 
     def state_size(buffer, send, recv):
-        piece = buffer.at[pl.ds(0, n_ctx - 1)]
-        return remote(piece, piece, send, recv, {"tensor": sib})
+        others_of = buffer.at[pl.ds(0, n_half - 1)]
+        return remote(others_of, others_of, send, recv, {"tensor": sib})
 
     state_size(rc1, p1_send, p1_recv).wait_recv()
-    running = jnp.zeros((chunk_rows, HEAD_DIM), F32)
-    for i in range(n_ctx):
+    half_copy = remote(after, before, half_send, half_recv, {"context": partner})
+
+    @pl.when(half == 1)
+    def _():
+        half_copy.wait_recv()
+
+    running = before[...]
+    for i in range(n_half):
         st2[i] = running.astype(BF16)
         running = running * edec[i : i + 1, :] + rc1[i].astype(F32)
+
+    @pl.when(half == 0)
+    def _():
+        after[...] = running
+        pl.semaphore_wait(ready, 1)
+        half_copy.start()
+
     for to in peers:
-        remote(st2.at[to], rc2.at[ctx], p2_send, p2_recv, {"context": to}).start()
-    rc2[pl.ds(ctx, 1)] = st2[pl.ds(ctx, 1)]
+        remote(
+            st2.at[to], rc2.at[piece], p2_send, p2_recv, {"context": first + to}
+        ).start()
+    rc2[pl.ds(piece, 1)] = st2[pl.ds(place, 1)]
 
     attend(1)
 
@@ -409,6 +446,11 @@
     state_size(st2, p2_send, p2_recv).wait_send()
     norm_copy.wait_send()
 
+    @pl.when(half == 0)
+    def _():
+        half_copy.wait_send()
+
+
     def finish_step(j, carry):
         finish_rows(j)
         return carry
@@ -422,7 +464,7 @@
 def body(n_ctx, activations, w_qkv, w_out, log_decay):
     rows, d_model = activations.shape
     width = HEADS * HEAD_DIM
-    chunk_rows = width // n_ctx
+    _, _, n_half, chunk_rows = split(n_ctx)
     hbm = pl.BlockSpec(memory_space=pltpu.HBM)
     vmem = pl.BlockSpec(memory_space=pltpu.VMEM)
     dma = pltpu.SemaphoreType.DMA
@@ -445,12 +487,14 @@
         pltpu.VMEM((2 * HEADS, BLOCK), F32),
         pltpu.VMEM((2 * HEADS, HEAD_DIM), F32),
         pltpu.VMEM((2 * HEADS, HEAD_DIM), F32),
-        pltpu.VMEM((n_ctx, 2 * HEADS, HEAD_DIM), F32),
-        pltpu.VMEM((n_ctx, HEAD_DIM), F32),
-        pltpu.VMEM((n_ctx, chunk_rows, HEAD_DIM), BF16),
-        pltpu.VMEM((n_ctx, chunk_rows, HEAD_DIM), BF16),
-        pltpu.VMEM((n_ctx, chunk_rows, HEAD_DIM), BF16),
-        pltpu.VMEM((n_ctx, chunk_rows, HEAD_DIM), BF16),
+        pltpu.VMEM((n_half, 2 * HEADS, HEAD_DIM), F32),
+        pltpu.VMEM((n_half, HEAD_DIM), F32),
+        pltpu.VMEM((n_half, chunk_rows, HEAD_DIM), BF16),
+        pltpu.VMEM((n_half, chunk_rows, HEAD_DIM), BF16),
+        pltpu.VMEM((n_half, chunk_rows, HEAD_DIM), BF16),
+        pltpu.VMEM((n_half, chunk_rows, HEAD_DIM), BF16),
+        pltpu.VMEM((chunk_rows, HEAD_DIM), F32),
+        pltpu.VMEM((chunk_rows, HEAD_DIM), F32),
         pltpu.VMEM((N_Y, rows, width), BF16),
         pltpu.VMEM((N_Y, rows, 2 * width), BF16),
         pltpu.VMEM((N_Y, rows, d_model), BF16),
@@ -483,6 +527,9 @@
         dma((OUT_CHUNKS,)),
         dma,
         dma,
+        dma,
+        dma,
+        pltpu.SemaphoreType.REGULAR,
     ]
     return pl.pallas_call(
         functools.partial(kernel, n_ctx),

time: 60.7 us -> 55.4 us (0.913)
  Pallas kernels: 59.8 us -> 54.5 us
    pallas_call x1, Pallas kernels: 59.8 us -> 54.5 us  [body(): pl.pallas_call(functools.partial(kernel, n_ctx), out_shape=jax.ShapeDtype...]
where the time goes in v4:
time: 55.4 us; the launch traced here: 55.3 us
  Pallas kernels  54.5 us (98%)
  local copies, waits for them, and re-layouts  0.75 us (1%)
    pallas_call x1, Pallas kernels, body(): pl.pallas_call(functools.partial(kernel, n_ctx), out_shape=jax.ShapeDtype...  54.5 us

profile of v4, /device:TPU:1, one launch (start us, length us, event | category | flops | bytes accessed | tf_op | source)
XLA Modules:
  0.0 55.3 jit_solution(16911411825002075691)
XLA Ops:
  0.0 54.5 %shard_map.46 = bf16[64,3072]{1,0:T(8,128)(2,1)S(1)} custom-call(bf16[64,3072]{1,0:T(8,128)(2,1)} %x_ref.1, bf16[3,3072,512]{2,1,0:T(8,128)(2,1)} %bitcast.1, bf16[512,3072]{1,0:T(8,128)(2,1)} %wo_ref.1, f32[4,512]{1,0:T(4,128)} %ld_ref.1), custom_call_target="tpu_custom_call" | custom-call | tf_op jit(solution)/shard_map/pallas_call | solution.py:534
  54.6 0.7 %copy.6 = bf16[64,3072]{1,0:T(8,128)(2,1)} copy(bf16[64,3072]{1,0:T(8,128)(2,1)S(1)} %shard_map.46) | data formatting | bytes 786432

commit v5 on v3

--- a/solution.py
+++ b/solution.py
@@ -12,7 +12,9 @@
 ROWS = 64
 HEADS = 4
 N_TENSOR = 8
+N_X = 4
 N_Y = 4
+GROUPS = 4
 IN_CHUNKS = (512,) * 6
 N_IN = len(IN_CHUNKS)
 OUT_CHUNKS = 6
@@ -28,14 +30,19 @@
     return half + half * jnp.tanh(half)
 
 
+def split(n_ctx):
+    n_in = n_ctx // GROUPS
+    return n_in, HEADS * HEAD_DIM // n_in
+
+
 def kernel(
     n_ctx, x_ref, w_ref, wo_ref, ld_ref, out_ref,
     xall, wv, w2, acc, qs_s, k_s, v_s, mask_s, eq_s, ek_s, inner_s, u_s,
     ld4, ld8, cum_s, elast_s, dsend, dec, edec,
-    st1, rc1, st2, rc2, nsend, nrm, part, relay, summed, from_b, from_f,
+    st1, rc1, st2, rc2, before, after, nsend, nrm, part, relay, summed, from_b, from_f,
     ag_send, ag_up, ag_down, ag_o, ag_s, ag_so, own_sem, w_sem, wo_own, wo_send, wo_recv,
     dec_send, dec_recv, p1_send, p1_recv, p2_send, p2_recv, n_send, n_recv,
-    rs_send, rs_relay, rs_b, rs_f, rs_sum_send, ld_sem,
+    rs_send, rs_relay, rs_b, rs_f, rs_sum_send, ld_sem, group_send, group_recv, ready,
 ):
     ctx = lax.axis_index("context")
     t = lax.axis_index("tensor")
@@ -45,20 +52,18 @@
     sib = y * 2 + other
     d_model = x_ref.shape[1]
     nc = d_model // OUT_CHUNKS
-    chunk_rows = HEADS * HEAD_DIM // n_ctx
-
-    n_x = 4
-    n_z = n_ctx // n_x
-
-    def hops(dz, dx):
-        return min(dz, n_z - dz) + min(dx, n_x - dx)
+
+    n_in, chunk_rows = split(n_ctx)
+    group, place = ctx // n_in, ctx % n_in
+    first = group * n_in
 
     others = sorted(
-        ((dz, dx) for dz in range(n_z) for dx in range(n_x) if dz or dx),
-        key=lambda d: -hops(*d),
+        ((dz, dx) for dz in range(n_in // N_X) for dx in range(N_X) if dz or dx),
+        key=lambda d: -(d[0] + min(d[1], N_X - d[1])),
     )
     peers = [
-        (ctx // n_x + dz) % n_z * n_x + (ctx % n_x + dx) % n_x for dz, dx in others
+        (place // N_X + dz) % (n_in // N_X) * N_X + (place % N_X + dx) % N_X
+        for dz, dx in others
     ]
 
     def remote(src, dst, send, recv, device):
@@ -165,18 +170,37 @@
             barrier, inc=1, device_id={"tensor": peer}, device_id_type=pl.DeviceIdType.MESH
         )
 
-    def greet(i, carry):
+    for to in peers:
         pl.semaphore_signal(
-            barrier, inc=1, device_id={"context": (ctx + i) % n_ctx},
+            barrier, inc=1, device_id={"context": first + to},
             device_id_type=pl.DeviceIdType.MESH,
         )
-        return carry
-
-    lax.fori_loop(1, n_ctx, greet, 0)
-    pl.semaphore_wait(barrier, 5 + n_ctx - 1)
+
+    for later_group in range(1, GROUPS):
+        @pl.when(later_group > group)
+        def _():
+            pl.semaphore_signal(
+                barrier, inc=1, device_id={"context": later_group * n_in + place},
+                device_id_type=pl.DeviceIdType.MESH,
+            )
+
+    pl.semaphore_wait(barrier, 5 + n_in - 1 + group)
 
     for j in range(N_IN):
         send_own(j)
+
+    for earlier in range(GROUPS - 1):
+        @pl.when(earlier < group)
+        def _():
+            pl.semaphore_signal(
+                ready.at[group], inc=1, device_id={"context": earlier * n_in + place},
+                device_id_type=pl.DeviceIdType.MESH,
+            )
+
+        @pl.when(earlier >= group)
+        def _():
+            before[earlier, 0:chunk_rows] = jnp.zeros((chunk_rows, HEAD_DIM), F32)
+            before[earlier, chunk_rows:] = jnp.ones((8, HEAD_DIM), F32)
 
     ld_copy.wait()
     ld8[0:HEADS, :] = ld4[:, 0:BLOCK]
@@ -192,15 +216,10 @@
     elast_s[...] = jnp.exp(last)
     both = last + pltpu.roll(last, HEADS, 0)
     dsend[...] = both
-    dec[pl.ds(ctx, 1)] = both[None]
-
-    def send_decay(i, carry):
-        remote(
-            dsend, dec.at[ctx], dec_send, dec_recv, {"context": (ctx + i) % n_ctx}
-        ).start()
-        return carry
-
-    lax.fori_loop(1, n_ctx, send_decay, 0)
+    dec[pl.ds(place, 1)] = both[None]
+
+    for to in peers:
+        remote(dsend, dec.at[place], dec_send, dec_recv, {"context": first + to}).start()
 
     def decay_tables(r):
         row = cum_s[pl.ds(r, 1), :]
@@ -229,13 +248,13 @@
 
     def decay_size():
         return remote(
-            dec.at[pl.ds(0, n_ctx - 1)], dec.at[pl.ds(0, n_ctx - 1)],
+            dec.at[pl.ds(0, n_in - 1)], dec.at[pl.ds(0, n_in - 1)],
             dec_send, dec_recv, {"tensor": sib},
         )
 
     decay_size().wait_recv()
-    my_head = ctx * chunk_rows // HEAD_DIM
-    for i in range(n_ctx):
+    my_head = place * chunk_rows // HEAD_DIM
+    for i in range(n_in):
         edec[i : i + 1, :] = jnp.exp(dec[i, pl.ds(my_head, 1), :])
 
     for j in range(EARLY, N_IN + EARLY):
@@ -270,8 +289,10 @@
         )
 
     for to in peers:
-        remote(st1.at[to], rc1.at[ctx], p1_send, p1_recv, {"context": to}).start()
-    rc1[pl.ds(ctx, 1)] = st1[pl.ds(ctx, 1)]
+        remote(
+            st1.at[to], rc1.at[place], p1_send, p1_recv, {"context": first + to}
+        ).start()
+    rc1[pl.ds(place, 1)] = st1[pl.ds(place, 1)]
 
     for j in range(N_IN):
         multiply(j, (OPPOSITE, 1), (0,))
@@ -294,17 +315,49 @@
     attend(0)
 
     def state_size(buffer, send, recv):
-        piece = buffer.at[pl.ds(0, n_ctx - 1)]
-        return remote(piece, piece, send, recv, {"tensor": sib})
+        others_of = buffer.at[pl.ds(0, n_in - 1)]
+        return remote(others_of, others_of, send, recv, {"tensor": sib})
 
     state_size(rc1, p1_send, p1_recv).wait_recv()
+    def group_copy(to):
+        return remote(
+            after, before.at[group], group_send.at[to], group_recv.at[group],
+            {"context": to * n_in + place},
+        )
+
     running = jnp.zeros((chunk_rows, HEAD_DIM), F32)
-    for i in range(n_ctx):
+    kept = jnp.ones((8, HEAD_DIM), F32)
+    for i in range(n_in):
+        running = running * edec[i : i + 1, :] + rc1[i].astype(F32)
+        kept = kept * edec[i : i + 1, :]
+    after[0:chunk_rows] = running
+    after[chunk_rows:] = kept
+    for later_group in range(1, GROUPS):
+        @pl.when(later_group > group)
+        def _():
+            pl.semaphore_wait(ready.at[later_group], 1)
+            group_copy(later_group).start()
+
+    running = jnp.zeros((chunk_rows, HEAD_DIM), F32)
+    for earlier in range(GROUPS - 1):
+        @pl.when(earlier < group)
+        def _():
+            remote(
+                before.at[earlier], before.at[earlier], group_send.at[0],
+                group_recv.at[earlier], {"tensor": sib},
+            ).wait_recv()
+
+        running = running * before[earlier, chunk_rows : chunk_rows + 1] + before[
+            earlier, 0:chunk_rows
+        ]
+    for i in range(n_in):
         st2[i] = running.astype(BF16)
         running = running * edec[i : i + 1, :] + rc1[i].astype(F32)
     for to in peers:
-        remote(st2.at[to], rc2.at[ctx], p2_send, p2_recv, {"context": to}).start()
-    rc2[pl.ds(ctx, 1)] = st2[pl.ds(ctx, 1)]
+        remote(
+            st2.at[to], rc2.at[place], p2_send, p2_recv, {"context": first + to}
+        ).start()
+    rc2[pl.ds(place, 1)] = st2[pl.ds(place, 1)]
 
     attend(1)
 
@@ -409,6 +462,12 @@
     state_size(st2, p2_send, p2_recv).wait_send()
     norm_copy.wait_send()
 
+    for later_group in range(1, GROUPS):
+        @pl.when(later_group > group)
+        def _():
+            group_copy(later_group).wait_send()
+
+
     def finish_step(j, carry):
         finish_rows(j)
         return carry
@@ -422,7 +481,7 @@
 def body(n_ctx, activations, w_qkv, w_out, log_decay):
     rows, d_model = activations.shape
     width = HEADS * HEAD_DIM
-    chunk_rows = width // n_ctx
+    n_in, chunk_rows = split(n_ctx)
     hbm = pl.BlockSpec(memory_space=pltpu.HBM)
     vmem = pl.BlockSpec(memory_space=pltpu.VMEM)
     dma = pltpu.SemaphoreType.DMA
@@ -445,12 +504,14 @@
         pltpu.VMEM((2 * HEADS, BLOCK), F32),
         pltpu.VMEM((2 * HEADS, HEAD_DIM), F32),
         pltpu.VMEM((2 * HEADS, HEAD_DIM), F32),
-        pltpu.VMEM((n_ctx, 2 * HEADS, HEAD_DIM), F32),
-        pltpu.VMEM((n_ctx, HEAD_DIM), F32),
-        pltpu.VMEM((n_ctx, chunk_rows, HEAD_DIM), BF16),
-        pltpu.VMEM((n_ctx, chunk_rows, HEAD_DIM), BF16),
-        pltpu.VMEM((n_ctx, chunk_rows, HEAD_DIM), BF16),
-        pltpu.VMEM((n_ctx, chunk_rows, HEAD_DIM), BF16),
+        pltpu.VMEM((n_in, 2 * HEADS, HEAD_DIM), F32),
+        pltpu.VMEM((n_in, HEAD_DIM), F32),
+        pltpu.VMEM((n_in, chunk_rows, HEAD_DIM), BF16),
+        pltpu.VMEM((n_in, chunk_rows, HEAD_DIM), BF16),
+        pltpu.VMEM((n_in, chunk_rows, HEAD_DIM), BF16),
+        pltpu.VMEM((n_in, chunk_rows, HEAD_DIM), BF16),
+        pltpu.VMEM((GROUPS - 1, chunk_rows + 8, HEAD_DIM), F32),
+        pltpu.VMEM((chunk_rows + 8, HEAD_DIM), F32),
         pltpu.VMEM((N_Y, rows, width), BF16),
         pltpu.VMEM((N_Y, rows, 2 * width), BF16),
         pltpu.VMEM((N_Y, rows, d_model), BF16),
@@ -483,6 +544,9 @@
         dma((OUT_CHUNKS,)),
         dma,
         dma,
+        dma((GROUPS,)),
+        dma((GROUPS,)),
+        pltpu.SemaphoreType.REGULAR((GROUPS,)),
     ]
     return pl.pallas_call(
         functools.partial(kernel, n_ctx),

time: 60.7 us -> 53.6 us (0.88)
  the two profiles are of different devices: /device:TPU:1 before, /device:TPU:225 now
where the time goes in v5:
time: 53.6 us; the launch traced here: 53.5 us
  Pallas kernels  52.7 us (98%)
  local copies, waits for them, and re-layouts  0.75 us (1%)
    pallas_call x1, Pallas kernels, body(): pl.pallas_call(functools.partial(kernel, n_ctx), out_shape=jax.ShapeDtype...  52.7 us

profile of v5, /device:TPU:225, one launch (start us, length us, event | category | flops | bytes accessed | tf_op | source)
XLA Modules:
  0.0 53.5 jit_solution(10271268319186905301)
XLA Ops:
  0.0 52.7 %shard_map.46 = bf16[64,3072]{1,0:T(8,128)(2,1)S(1)} custom-call(bf16[64,3072]{1,0:T(8,128)(2,1)} %x_ref.1, bf16[3,3072,512]{2,1,0:T(8,128)(2,1)} %bitcast.1, bf16[512,3072]{1,0:T(8,128)(2,1)} %wo_ref.1, f32[4,512]{1,0:T(4,128)} %ld_ref.1), custom_call_target="tpu_custom_call" | custom-call | tf_op jit(solution)/shard_map/pallas_call | solution.py:551
  52.8 0.7 %copy.6 = bf16[64,3072]{1,0:T(8,128)(2,1)} copy(bf16[64,3072]{1,0:T(8,128)(2,1)S(1)} %shard_map.46) | data formatting | bytes 786432

commit v6 on v5

--- a/solution.py
+++ b/solution.py
@@ -156,6 +156,11 @@
     def block_of(i, n, lanes):
         return jnp.concatenate([rows_of(i, 2 * n, lanes), rows_of(i, 2 * n + 1, lanes)], axis=0)
 
+    def two_parts(value):
+        high = value.astype(BF16).astype(F32)
+        row = lax.broadcasted_iota(jnp.int32, (16, HEAD_DIM), 0)
+        return jnp.where(row < 8, high, value - high).astype(BF16)
+
     ld_copy = pltpu.make_async_copy(ld_ref, ld4, ld_sem)
     ld_copy.start()
     for j in range(N_IN):
@@ -199,8 +204,8 @@
 
         @pl.when(earlier >= group)
         def _():
-            before[earlier, 0:chunk_rows] = jnp.zeros((chunk_rows, HEAD_DIM), F32)
-            before[earlier, chunk_rows:] = jnp.ones((8, HEAD_DIM), F32)
+            before[earlier, 0:chunk_rows] = jnp.zeros((chunk_rows, HEAD_DIM), BF16)
+            before[earlier, chunk_rows:] = two_parts(jnp.ones((16, HEAD_DIM), F32))
 
     ld_copy.wait()
     ld8[0:HEADS, :] = ld4[:, 0:BLOCK]
@@ -326,12 +331,12 @@
         )
 
     running = jnp.zeros((chunk_rows, HEAD_DIM), F32)
-    kept = jnp.ones((8, HEAD_DIM), F32)
+    kept = jnp.ones((16, HEAD_DIM), F32)
     for i in range(n_in):
         running = running * edec[i : i + 1, :] + rc1[i].astype(F32)
         kept = kept * edec[i : i + 1, :]
-    after[0:chunk_rows] = running
-    after[chunk_rows:] = kept
+    after[0:chunk_rows] = running.astype(BF16)
+    after[chunk_rows:] = two_parts(kept)
     for later_group in range(1, GROUPS):
         @pl.when(later_group > group)
         def _():
@@ -347,9 +352,8 @@
                 group_recv.at[earlier], {"tensor": sib},
             ).wait_recv()
 
-        running = running * before[earlier, chunk_rows : chunk_rows + 1] + before[
-            earlier, 0:chunk_rows
-        ]
+        parts = before[earlier, chunk_rows:].astype(F32)
+        running = running * (parts[0:1] + parts[8:9]) + before[earlier, 0:chunk_rows].astype(F32)
     for i in range(n_in):
         st2[i] = running.astype(BF16)
         running = running * edec[i : i + 1, :] + rc1[i].astype(F32)
@@ -510,8 +514,8 @@
         pltpu.VMEM((n_in, chunk_rows, HEAD_DIM), BF16),
         pltpu.VMEM((n_in, chunk_rows, HEAD_DIM), BF16),
         pltpu.VMEM((n_in, chunk_rows, HEAD_DIM), BF16),
-        pltpu.VMEM((GROUPS - 1, chunk_rows + 8, HEAD_DIM), F32),
-        pltpu.VMEM((chunk_rows + 8, HEAD_DIM), F32),
+        pltpu.VMEM((GROUPS - 1, chunk_rows + 16, HEAD_DIM), BF16),
+        pltpu.VMEM((chunk_rows + 16, HEAD_DIM), BF16),
         pltpu.VMEM((N_Y, rows, width), BF16),
         pltpu.VMEM((N_Y, rows, 2 * width), BF16),
         pltpu.VMEM((N_Y, rows, d_model), BF16),

time: 53.6 us -> 52.2 us (0.974)
  the two profiles are of different devices: /device:TPU:225 before, /device:TPU:193 now
where the time goes in v6:
time: 52.2 us; the launch traced here: 52.1 us
  Pallas kernels  51.4 us (98%)
  local copies, waits for them, and re-layouts  0.75 us (1%)
    pallas_call x1, Pallas kernels, body(): pl.pallas_call(functools.partial(kernel, n_ctx), out_shape=jax.ShapeDtype...  51.4 us

profile of v6, /device:TPU:193, one launch (start us, length us, event | category | flops | bytes accessed | tf_op | source)
XLA Modules:
  0.0 52.1 jit_solution(17694283362554852891)
XLA Ops:
  0.0 51.4 %shard_map.46 = bf16[64,3072]{1,0:T(8,128)(2,1)S(1)} custom-call(bf16[64,3072]{1,0:T(8,128)(2,1)} %x_ref.1, bf16[3,3072,512]{2,1,0:T(8,128)(2,1)} %bitcast.1, bf16[512,3072]{1,0:T(8,128)(2,1)} %wo_ref.1, f32[4,512]{1,0:T(4,128)} %ld_ref.1), custom_call_target="tpu_custom_call" | custom-call | tf_op jit(solution)/shard_map/pallas_call | solution.py:555
  51.4 0.7 %copy.6 = bf16[64,3072]{1,0:T(8,128)(2,1)} copy(bf16[64,3072]{1,0:T(8,128)(2,1)S(1)} %shard_map.46) | data formatting | bytes 786432

commit v7 on v6

--- a/solution.py
+++ b/solution.py
@@ -15,7 +15,7 @@
 N_X = 4
 N_Y = 4
 GROUPS = 4
-IN_CHUNKS = (512,) * 6
+IN_CHUNKS = (512, 512, 512, 512, 512, 256, 256)
 N_IN = len(IN_CHUNKS)
 OUT_CHUNKS = 6
 LAG = 3

time: 52.2 us -> 52 us (level)
  the two profiles are of different devices: /device:TPU:193 before, /device:TPU:225 now
where the time goes in v7:
time: 52 us; the launch traced here: 51.9 us
  Pallas kernels  51.1 us (98%)
  local copies, waits for them, and re-layouts  0.75 us (1%)
    pallas_call x1, Pallas kernels, body(): pl.pallas_call(functools.partial(kernel, n_ctx), out_shape=jax.ShapeDtype...  51.1 us

profile of v7, /device:TPU:225, one launch (start us, length us, event | category | flops | bytes accessed | tf_op | source)
XLA Modules:
  0.0 51.9 jit_solution(16937415420566592709)
XLA Ops:
  0.0 51.1 %shard_map.46 = bf16[64,3072]{1,0:T(8,128)(2,1)S(1)} custom-call(bf16[64,3072]{1,0:T(8,128)(2,1)} %x_ref.1, bf16[3,3072,512]{2,1,0:T(8,128)(2,1)} %bitcast.1, bf16[512,3072]{1,0:T(8,128)(2,1)} %wo_ref.1, f32[4,512]{1,0:T(4,128)} %ld_ref.1), custom_call_target="tpu_custom_call" | custom-call | tf_op jit(solution)/shard_map/pallas_call | solution.py:555
  51.2 0.7 %copy.6 = bf16[64,3072]{1,0:T(8,128)(2,1)} copy(bf16[64,3072]{1,0:T(8,128)(2,1)S(1)} %shard_map.46) | data formatting | bytes 786432

commit v8 on v7

--- a/solution.py
+++ b/solution.py
@@ -19,7 +19,7 @@
 N_IN = len(IN_CHUNKS)
 OUT_CHUNKS = 6
 LAG = 3
-EARLY = 2
+EARLY = 3
 OWN, UP, DOWN, OPPOSITE = range(N_Y)
 F32 = jnp.float32
 BF16 = jnp.bfloat16
@@ -118,7 +118,7 @@
         src = xall.at[UP + upward, core, :, cols]
         dst = xall.at[OPPOSITE, core, :, cols]
         remote(src, dst, ag_send, ag_o.at[j], {"tensor": chip + core}).start()
-        if j == N_IN - 1:
+        if j >= N_IN - 2:
             remote(src, dst, ag_send, ag_so.at[j], {"tensor": chip + other}).start()
         near = xall.at[pl.ds(UP, 2), core, :, cols]
         remote(near, near, ag_send, ag_s.at[j], {"tensor": sib}).start()
@@ -126,7 +126,7 @@
     def pass_opposite(j):
         ref = xall.at[OPPOSITE, core, :, in_cols(j)]
         arrived(ref, ag_o.at[j])
-        if j < N_IN - 1:
+        if j < N_IN - 2:
             remote(ref, ref, ag_send, ag_so.at[j], {"tensor": sib}).start()
 
     def multiply(j, slots, parts):

time: 52 us -> 52.4 us (level)
  no operation moved by 1% of the time
where the time goes in v8:
time: 52.4 us; the launch traced here: 52.3 us
  Pallas kernels  51.6 us (98%)
  local copies, waits for them, and re-layouts  0.75 us (1%)
    pallas_call x1, Pallas kernels, body(): pl.pallas_call(functools.partial(kernel, n_ctx), out_shape=jax.ShapeDtype...  51.6 us

profile of v8, /device:TPU:225, one launch (start us, length us, event | category | flops | bytes accessed | tf_op | source)
XLA Modules:
  0.0 52.3 jit_solution(12533291213383438241)
XLA Ops:
  0.0 51.6 %shard_map.46 = bf16[64,3072]{1,0:T(8,128)(2,1)S(1)} custom-call(bf16[64,3072]{1,0:T(8,128)(2,1)} %x_ref.1, bf16[3,3072,512]{2,1,0:T(8,128)(2,1)} %bitcast.1, bf16[512,3072]{1,0:T(8,128)(2,1)} %wo_ref.1, f32[4,512]{1,0:T(4,128)} %ld_ref.1), custom_call_target="tpu_custom_call" | custom-call | tf_op jit(solution)/shard_map/pallas_call | solution.py:555
  51.6 0.7 %copy.6 = bf16[64,3072]{1,0:T(8,128)(2,1)} copy(bf16[64,3072]{1,0:T(8,128)(2,1)S(1)} %shard_map.46) | data formatting | bytes 786432
